TPU v7x, 32 devices: a whole 2x2x4 slice. The times are simulated.
32 devices in a mesh: section: 2 (over y), dp: 8 (over z, x), tensor: 2 (over core).
Axes of the slice: x: 2, y: 2, z: 4, core: 2. Of those that a mesh axis runs over, the one named last changes fastest.
Arguments:
- chain_inputs: bfloat16 [7680, 768], P('dp', 'tensor'), may hold values from -6 to 6
- cotangent: bfloat16 [7680, 768], P('dp', 'tensor'), may hold values from -6 to 6
- chain_tags: int32 [48], P('dp'), may hold values 0 or 1
- pad_mask: int32 [7680], P('dp'), may hold values from 0 to 1, as said below
- predicted: int32 [7680], P('dp'), may hold values from 0 to 23
- target_ids: int32 [7680], P('dp'), may hold values from 0 to 23
- joint_proj: bfloat16 [2, 2, 768, 3, 768], P('section', None, None, None, 'tensor'), may hold values from -0.21875 to 0.21875
- output_proj: bfloat16 [2, 2, 768, 768], P('section', None, 'tensor'), may hold values from -0.875 to 0.875
- up_proj: bfloat16 [2, 2, 768, 3072], P('section', None, None, 'tensor'), may hold values from -0.21875 to 0.21875
- up_bias: bfloat16 [2, 2, 3072], P('section', None, 'tensor'), may hold values from -3 to 3
- down_proj: bfloat16 [2, 2, 3072, 768], P('section', None, 'tensor'), may hold values from -0.109375 to 0.109375
- norm_gain: float32 [2, 2, 768], P('section'), may hold values from 0.25 to 1.75
- norm_shift: float32 [2, 2, 768], P('section'), may hold values from -2 to 2
Outputs:
- layer_outputs: bfloat16 [2, 7680, 768], P('section', 'dp', 'tensor')
- input_grads: float32 [2, 7680, 768], P('section', 'dp', 'tensor')
- joint_grad: float32 [2, 2, 768, 3, 768], P('section', None, None, None, 'tensor')
- output_grad: float32 [2, 2, 768, 768], P('section', None, 'tensor')
- up_grad: float32 [2, 2, 768, 3072], P('section', None, None, 'tensor')
- bias_grad: float32 [2, 2, 3072], P('section', None, 'tensor')
- down_grad: float32 [2, 2, 3072, 768], P('section', None, 'tensor')
- gain_grad: float32 [2, 2, 768], P('section')
- shift_grad: float32 [2, 2, 768], P('section')
- residue_counts: int32 [2, 24], replicated
Inputs may be any that keep to these rules, and one draw needn't show every extreme that they name: `pad_mask`: each chain's live positions are its first ones, at least 40 of them; some chains are padded.
All inputs are finite; a program needn't handle non-finite values. No bound on the sum of `chain_tags` on one device may be relied on, other than what follows from the above.
Results may differ from a plain program's by a relative error of at most 0.035.
Values may be sent and summed in bfloat16 or wider, within the bound.
No kernel may reach another device: no remote copies, remote signals or barrier semaphores. Data moves between devices by JAX's collectives and lax.ppermute only.
A program may use at most 256 MiB of HBM per device.

v0:
```python
import jax
import jax.numpy as jnp
from jax import lax
from jax.sharding import PartitionSpec as P

HEAD_DIM = 64
SYMBOLS = 24
SEQ = 160
MB = 2


root_half = 0.7071067811865476
root_two_pi = 0.3989422804014327


def from_behind(value, axis, steps):
    count = lax.axis_size(axis)
    leading, last = (max(0, -steps), min(count, count - steps))
    return lax.ppermute(value, axis, [(source, source + steps) for source in range(leading, last)])


def pick_product(rows, weights, is_light):
    first_set = jnp.dot(rows, weights[0], preferred_element_type=jnp.float32)
    second_set = jnp.dot(rows, weights[1], preferred_element_type=jnp.float32)
    return jnp.where(is_light, second_set, first_set)


def back_product(grads, weights, is_light):
    contract_cols = (((1,), (1,)), ((), ()))
    first_set = lax.dot_general(
        grads, weights[0], contract_cols, preferred_element_type=jnp.float32
    )
    second_set = lax.dot_general(
        grads, weights[1], contract_cols, preferred_element_type=jnp.float32
    )
    return jnp.where(is_light, second_set, first_set)


def weight_pair(rows, grads, is_light):
    contract_rows = (((0,), (0,)), ((), ()))
    zero_rows = jnp.zeros_like(rows)
    heavy_rows = jnp.where(is_light, zero_rows, rows)
    light_rows = jnp.where(is_light, rows, zero_rows)
    first_set = lax.dot_general(
        heavy_rows, grads, contract_rows, preferred_element_type=jnp.float32
    )
    second_set = lax.dot_general(
        light_rows, grads, contract_rows, preferred_element_type=jnp.float32
    )
    return jnp.stack([first_set, second_set])


def layer_norm(rows, gain, shift):
    centred = rows - jnp.mean(rows, axis=-1, keepdims=True)
    inv_root = lax.rsqrt(jnp.mean(centred * centred, axis=-1, keepdims=True) + 1e-05)
    normal = centred * inv_root
    return (normal * gain + shift, normal, inv_root)


def norm_back(grads, normal, inv_root, gain):
    scaled = grads * gain
    inner = (
        scaled
        - jnp.mean(scaled, axis=-1, keepdims=True)
        - normal * jnp.mean(scaled * normal, axis=-1, keepdims=True)
    )
    return (inner * inv_root, jnp.sum(grads * normal, 0), jnp.sum(grads, 0))


def layer_forward(rows_in, is_light, key_live, params):
    joint, output, up_w, up_b, down_w, gains, shifts = params
    rows_count = rows_in.shape[0]
    chains = key_live.shape[0]
    local_heads = output.shape[1] // HEAD_DIM
    joined = pick_product(rows_in, joint, is_light).astype(jnp.bfloat16)
    pieces = joined.reshape(chains, SEQ, 3, local_heads, HEAD_DIM)
    queries = pieces[:, :, 0]
    key_rows = pieces[:, :, 1]
    values = pieces[:, :, 2]
    raw_scores = jnp.einsum(
        "cqhd,ckhd->chqk", queries, key_rows, preferred_element_type=jnp.float32
    )
    scores = jnp.where(key_live[:, None, None, :], raw_scores * HEAD_DIM ** (-0.5), -1000000000.0)
    shifted = jnp.exp(scores - jnp.max(scores, axis=-1, keepdims=True))
    attn_probs = shifted / jnp.sum(shifted, axis=-1, keepdims=True)
    probs_low = attn_probs.astype(jnp.bfloat16)
    mixed_heads = jnp.einsum(
        "chqk,ckhd->cqhd", probs_low, values, preferred_element_type=jnp.float32
    )
    mixed_heads = mixed_heads.astype(jnp.bfloat16).reshape(rows_count, -1)
    attn_total = lax.psum(pick_product(mixed_heads, output, is_light), "tensor")
    normed_one, normal_one, root_one = layer_norm(
        rows_in.astype(jnp.float32) + attn_total, gains[0], shifts[0]
    )
    normed_low = normed_one.astype(jnp.bfloat16)
    pre_act = pick_product(normed_low, up_w, is_light) + jnp.where(
        is_light, up_b[1], up_b[0]
    ).astype(jnp.float32)
    hidden = jax.nn.gelu(pre_act, approximate=False).astype(jnp.bfloat16)
    down_total = lax.psum(
        pick_product(hidden, down_w, is_light).astype(jnp.bfloat16), "tensor"
    ).astype(jnp.float32)
    result, normal_two, root_two = layer_norm(normed_one + down_total, gains[1], shifts[1])
    kept = (
        queries,
        key_rows,
        values,
        attn_probs,
        probs_low,
        mixed_heads,
        normal_one,
        root_one,
        normed_low,
        pre_act,
        hidden,
        normal_two,
        root_two,
    )
    return (result, kept)


def feed_backward(grad_out, kept, is_light, params):
    joint, output, up_w, up_b, down_w, gains, shifts = params
    normed_low, pre_act, hidden, normal_two, root_two = (
        kept[8],
        kept[9],
        kept[10],
        kept[11],
        kept[12],
    )
    grad_two, gain_two, shift_two = norm_back(grad_out, normal_two, root_two, gains[1])
    down_low = grad_two.astype(jnp.bfloat16)
    down_grad = weight_pair(hidden, down_low, is_light)
    hidden_grad = back_product(down_low, down_w, is_light)
    gelu_slope = (
        0.5 * (1.0 + lax.erf(pre_act * root_half))
        + pre_act * jnp.exp(-0.5 * pre_act * pre_act) * root_two_pi
    )
    pre_low = (hidden_grad * gelu_slope).astype(jnp.bfloat16)
    up_grad = weight_pair(normed_low, pre_low, is_light)
    pre_wide = pre_low.astype(jnp.float32)
    zero_wide = jnp.zeros_like(pre_wide)
    bias_grad = jnp.stack(
        [
            jnp.sum(jnp.where(is_light, zero_wide, pre_wide), 0),
            jnp.sum(jnp.where(is_light, pre_wide, zero_wide), 0),
        ]
    )
    normed_grad = grad_two + lax.psum(
        back_product(pre_low, up_w, is_light).astype(jnp.bfloat16), "tensor"
    ).astype(jnp.float32)
    return (normed_grad, (down_grad, up_grad, bias_grad, gain_two, shift_two))


def mixer_backward(normed_grad, kept, rows_in, is_light, params):
    joint, output, up_w, up_b, down_w, gains, shifts = params
    queries, key_rows, values, attn_probs, probs_low, mixed_heads, normal_one, root_one = kept[:8]
    grad_one, gain_one, shift_one = norm_back(normed_grad, normal_one, root_one, gains[0])
    attn_low = grad_one.astype(jnp.bfloat16)
    output_grad = weight_pair(mixed_heads, attn_low, is_light)
    mixed_grad = (
        back_product(attn_low, output, is_light).astype(jnp.bfloat16).reshape(queries.shape)
    )
    probs_grad = jnp.einsum(
        "cqhd,ckhd->chqk", mixed_grad, values, preferred_element_type=jnp.float32
    )
    score_low = (
        attn_probs * (probs_grad - jnp.sum(attn_probs * probs_grad, axis=-1, keepdims=True))
    ).astype(jnp.bfloat16)
    query_grad = jnp.einsum(
        "chqk,ckhd->cqhd", score_low, key_rows, preferred_element_type=jnp.float32
    ) * HEAD_DIM ** (-0.5)
    key_grad = jnp.einsum(
        "chqk,cqhd->ckhd", score_low, queries, preferred_element_type=jnp.float32
    ) * HEAD_DIM ** (-0.5)
    value_grad = jnp.einsum(
        "chqk,cqhd->ckhd", probs_low, mixed_grad, preferred_element_type=jnp.float32
    )
    joined_grad = (
        jnp.stack([query_grad, key_grad, value_grad], axis=2)
        .astype(jnp.bfloat16)
        .reshape(rows_in.shape[0], -1)
    )
    joint_grad = weight_pair(rows_in, joined_grad, is_light)
    input_grad = grad_one + lax.psum(
        back_product(joined_grad, joint, is_light).astype(jnp.bfloat16), "tensor"
    ).astype(jnp.float32)
    return (input_grad, (joint_grad, output_grad, gain_one, shift_one))


def shards(
    chain_inputs,
    cotangent,
    chain_tags,
    pad_mask,
    predicted,
    target_ids,
    joint_proj,
    output_proj,
    up_proj,
    up_bias,
    down_proj,
    norm_gain,
    norm_shift,
):
    section_rank = lax.axis_index("section")
    tensor_rank = lax.axis_index("tensor")
    full_rows, full_cot = (
        lax.all_gather(chain_inputs, "tensor", axis=1, tiled=True),
        lax.all_gather(cotangent, "tensor", axis=1, tiled=True),
    )
    tokens = full_rows.shape[0]
    model_width = full_rows.shape[1]
    batch_rows = tokens // MB
    chains = batch_rows // SEQ
    rows_split = full_rows.reshape(MB, batch_rows, model_width)
    cot_split = full_cot.reshape(MB, batch_rows, model_width)
    light_split = (jnp.repeat(chain_tags, SEQ) > 0).reshape(MB, batch_rows, 1)
    live_split = (pad_mask > 0).reshape(MB, chains, SEQ)
    joint = joint_proj[0].reshape(2, model_width, -1)
    params = (
        joint,
        output_proj[0],
        up_proj[0],
        up_bias[0],
        down_proj[0],
        norm_gain[0],
        norm_shift[0],
    )
    kept_inputs = jnp.zeros((MB, batch_rows, model_width), jnp.bfloat16)
    kept_outputs = jnp.zeros((MB, batch_rows, model_width), jnp.bfloat16)
    arriving = jnp.zeros((batch_rows, model_width), jnp.bfloat16)
    for moment in range(MB + 1):
        batch_index = moment - section_rank
        active = (batch_index >= 0) & (batch_index < MB)
        slot_index = jnp.clip(batch_index, 0, MB - 1)
        own_rows = lax.dynamic_index_in_dim(rows_split, slot_index, 0, keepdims=False)
        rows_in = jnp.where(section_rank == 0, own_rows, arriving)
        is_light = lax.dynamic_index_in_dim(light_split, slot_index, 0, keepdims=False)
        key_live = lax.dynamic_index_in_dim(live_split, slot_index, 0, keepdims=False)
        result, unused_kept = layer_forward(rows_in, is_light, key_live, params)
        result_low = result.astype(jnp.bfloat16)
        kept_inputs = jnp.where(
            active,
            lax.dynamic_update_index_in_dim(kept_inputs, rows_in, slot_index, 0),
            kept_inputs,
        )
        kept_outputs = jnp.where(
            active,
            lax.dynamic_update_index_in_dim(kept_outputs, result_low, slot_index, 0),
            kept_outputs,
        )
        if moment < MB:
            arriving = from_behind(result_low, "section", 1)
    symbols = jnp.arange(SYMBOLS, dtype=jnp.int32)
    target_hits = (target_ids[:, None] == symbols[None, :]) & (pad_mask[:, None] > 0)
    correct_hits = target_hits & (predicted == target_ids)[:, None]
    counts_wide = jnp.stack([jnp.sum(target_hits, 0), jnp.sum(correct_hits, 0)]).astype(jnp.float32)
    kept_grads = jnp.zeros((MB, batch_rows, model_width), jnp.float32)
    arriving = jnp.zeros((batch_rows, model_width), jnp.bfloat16)
    feed_totals = None
    mixer_totals = None
    for moment in range(MB + 1):
        batch_index = moment - 1 + section_rank
        active = (batch_index >= 0) & (batch_index < MB)
        slot_index = jnp.clip(batch_index, 0, MB - 1)
        rows_in = lax.dynamic_index_in_dim(kept_inputs, slot_index, 0, keepdims=False)
        own_cot = lax.dynamic_index_in_dim(cot_split, slot_index, 0, keepdims=False).astype(
            jnp.float32
        )
        grad_out = jnp.where(section_rank == 1, own_cot, arriving.astype(jnp.float32))
        grad_out = jnp.where(active, grad_out, jnp.zeros_like(grad_out))
        is_light = lax.dynamic_index_in_dim(light_split, slot_index, 0, keepdims=False)
        key_live = lax.dynamic_index_in_dim(live_split, slot_index, 0, keepdims=False)
        result, kept = layer_forward(rows_in, is_light, key_live, params)
        normed_grad, feed_part = feed_backward(grad_out, kept, is_light, params)
        feed_totals = (
            feed_part if feed_totals is None else jax.tree.map(jnp.add, feed_totals, feed_part)
        )
        input_grad, mixer_part = mixer_backward(normed_grad, kept, rows_in, is_light, params)
        mixer_totals = (
            mixer_part if mixer_totals is None else jax.tree.map(jnp.add, mixer_totals, mixer_part)
        )
        kept_grads = jnp.where(
            active,
            lax.dynamic_update_index_in_dim(kept_grads, input_grad, slot_index, 0),
            kept_grads,
        )
        if moment < MB:
            arriving = from_behind(input_grad.astype(jnp.bfloat16), "section", -1)
    (
        joint_sum,
        output_sum,
        gain_one,
        shift_one,
        down_sum,
        up_sum,
        bias_sum,
        gain_two,
        shift_two,
        count_sum,
    ) = (
        lax.psum(mixer_totals[0].astype(jnp.bfloat16), "dp").astype(jnp.float32),
        lax.psum(mixer_totals[1].astype(jnp.bfloat16), "dp").astype(jnp.float32),
        lax.psum(mixer_totals[2].astype(jnp.bfloat16), "dp").astype(jnp.float32),
        lax.psum(mixer_totals[3].astype(jnp.bfloat16), "dp").astype(jnp.float32),
        lax.psum(feed_totals[0].astype(jnp.bfloat16), "dp").astype(jnp.float32),
        lax.psum(feed_totals[1].astype(jnp.bfloat16), "dp").astype(jnp.float32),
        lax.psum(feed_totals[2].astype(jnp.bfloat16), "dp").astype(jnp.float32),
        lax.psum(feed_totals[3].astype(jnp.bfloat16), "dp").astype(jnp.float32),
        lax.psum(feed_totals[4].astype(jnp.bfloat16), "dp").astype(jnp.float32),
        lax.psum(counts_wide.astype(jnp.bfloat16), "dp").astype(jnp.float32),
    )
    columns = model_width // lax.axis_size("tensor")
    col_start = tensor_rank * columns
    layer_outputs = lax.dynamic_slice_in_dim(
        kept_outputs.reshape(tokens, model_width), col_start, columns, 1
    )[None]
    input_grads = lax.dynamic_slice_in_dim(
        kept_grads.reshape(tokens, model_width), col_start, columns, 1
    )[None]
    return (
        layer_outputs,
        input_grads,
        joint_sum.reshape(joint_proj.shape),
        output_sum[None],
        up_sum[None],
        bias_sum[None],
        down_sum[None],
        jnp.stack([gain_one, gain_two])[None],
        jnp.stack([shift_one, shift_two])[None],
        count_sum.astype(jnp.int32),
    )


def solution(mesh):
    return jax.shard_map(
        shards,
        mesh=mesh,
        in_specs=(
            P("dp", "tensor"),
            P("dp", "tensor"),
            P("dp"),
            P("dp"),
            P("dp"),
            P("dp"),
            P("section", None, None, None, "tensor"),
            P("section", None, "tensor", None),
            P("section", None, None, "tensor"),
            P("section", None, "tensor"),
            P("section", None, "tensor", None),
            P("section", None, None),
            P("section", None, None),
        ),
        out_specs=(
            P("section", "dp", "tensor"),
            P("section", "dp", "tensor"),
            P("section", None, None, None, "tensor"),
            P("section", None, "tensor", None),
            P("section", None, None, "tensor"),
            P("section", None, "tensor"),
            P("section", None, "tensor", None),
            P("section", None, None),
            P("section", None, None),
            P(),
        ),
        check_vma=False,
    )
```

profile of v0, /device:TPU:0, one launch (start us, length us, event | category | flops | bytes accessed | tf_op | source)
XLA Modules:
  0.0 1293.8 jit_solution(6218583309858273989)
XLA Ops:
  46.7 21.1 %all-reduce.20.cloned.1.call-done = f32[480,768]{1,0:T(8,128)} async-done(((f32[480,768]{1,0:T(8,128)}), f32[480,768]{1,0:T(8,128)}) %all-reduce.20.cloned.1.call-update) | async-done | bytes 1474576 | tf_op jit(solution)/shard_map/psum | solution.py:91
  75.0 9.1 fusion.31
  87.7 20.4 %all-reduce.22.cloned.1.call-done = bf16[480,768]{1,0:T(8,128)(2,1)} async-done(((bf16[480,768]{1,0:T(8,128)(2,1)}), bf16[480,768]{1,0:T(8,128)(2,1)}) %all-reduce.22.cloned.1.call-update) | async-done | bytes 737296 | tf_op jit(solution)/shard_map/psum | solution.py:100
  119.8 13.6 %collective-permute-done = bf16[480,768]{1,0:T(8,128)(2,1)} collective-permute-done((bf16[480,768]{1,0:T(8,128)(2,1)}, bf16[480,768]{1,0:T(8,128)(2,1)}, u32[]{:S(2)}, u32[]{:S(2)}) %collective-permute-start) | collective-permute-done | bytes 737312 | tf_op jit(solution)/shard_map/ppermute | solution.py:19
  160.8 23.2 %all-reduce.24.cloned.1.call-done = f32[480,768]{1,0:T(8,128)} async-done(((f32[480,768]{1,0:T(8,128)}), f32[480,768]{1,0:T(8,128)}) %all-reduce.24.cloned.1.call-update) | async-done | bytes 1474576 | tf_op jit(solution)/shard_map/psum | solution.py:91
  190.2 9.1 fusion.34
  202.9 20.4 %all-reduce.26.cloned.1.call-done = bf16[480,768]{1,0:T(8,128)(2,1)} async-done(((bf16[480,768]{1,0:T(8,128)(2,1)}), bf16[480,768]{1,0:T(8,128)(2,1)}) %all-reduce.26.cloned.1.call-update) | async-done | bytes 737296 | tf_op jit(solution)/shard_map/psum | solution.py:100
  233.1 15.6 %collective-permute-done.1 = bf16[480,768]{1,0:T(8,128)(2,1)} collective-permute-done((bf16[480,768]{1,0:T(8,128)(2,1)}, bf16[480,768]{1,0:T(8,128)(2,1)}, u32[]{:S(2)}, u32[]{:S(2)}) %collective-permute-start.1) | collective-permute-done | bytes 737312 | tf_op jit(solution)/shard_map/ppermute | solution.py:19
  370.2 33.7 %all-reduce.36.cloned.1.call-done = (f32[480,768]{1,0:T(8,128)}, f32[480,768]{1,0:T(8,128)}, f32[480,768]{1,0:T(8,128)}, f32[480,768]{1,0:T(8,128)}) async-done(((f32[480,768]{1,0:T(8,128)}, f32[480,768]{1,0:T(8,128)}, f32[480,768]{1,0:T(8,128)}, f32[480,768]{1,0:T(8,128)}), (f32[480,768]{1,0:T(8,128)}, f32[480,768]{1,0:T(8,128)}, f32[480,768]{1,0:T(8,128)}, ...) | async-done | bytes 5898256 | tf_op jit(solution)/shard_map/psum | solution.py:91
  409.6 9.1 fusion.40
  432.7 10.0 all-reduce.28.cloned.1.call-done
  447.4 7.9 all-gather.5.cloned.1.call-done
  469.5 9.4 fusion.47
  498.0 10.4 all-reduce.30.cloned.1.call-done
  566.5 10.4 fusion.54
  581.0 16.7 %collective-permute-done.2 = bf16[480,768]{1,0:T(8,128)(2,1)S(1)} collective-permute-done((bf16[480,768]{1,0:T(8,128)(2,1)S(1)}, bf16[480,768]{1,0:T(8,128)(2,1)S(1)}, u32[]{:S(2)}, u32[]{:S(2)}) %collective-permute-start.2) | collective-permute-done | bytes 737312 | tf_op jit(solution)/shard_map/ppermute | solution.py:19
  622.1 7.1 all-reduce.32.cloned.1.call-done
  683.6 9.1 fusion.37
  698.6 16.3 %collective-permute-done.3 = bf16[480,768]{1,0:T(8,128)(2,1)S(1)} collective-permute-done((bf16[480,768]{1,0:T(8,128)(2,1)S(1)}, bf16[480,768]{1,0:T(8,128)(2,1)S(1)}, u32[]{:S(2)}, u32[]{:S(2)}) %collective-permute-start.3) | collective-permute-done | bytes 737312 | tf_op jit(solution)/shard_map/ppermute | solution.py:19
  741.6 12.8 fusion.13
  754.4 12.4 fusion.12
  825.5 39.9 %all-reduce.1 = (bf16[1,2,1536]{2,1,0:T(2,128)(2,1)S(1)}, bf16[1,768]{1,0:T(2,128)(2,1)S(1)}, bf16[1,768]{1,0:T(2,128)(2,1)S(1)}, bf16[1,768]{1,0:T(2,128)(2,1)S...) all-reduce(bf16[1,2,1536]{2,1,0:T(2,128)(2,1)S(1)} %fusion.522, ...), channel_id=1, replica_groups=mesh['section'=2,'dp'=8,'tensor'=2] {'dp'}, use_global_device_ids=true, to_apply=%region_78.79 | all-reduce | flops 6192 | bytes 24768 | tf_op jit(solution)/shard_map/psum | solution.py:309
  877.3 389.2 %all-reduce.38.cloned.1.call-done = (bf16[1,2,768,3,384]{2,4,3,1,0:T(8,128)(2,1)}, bf16[1,2,384,768]{3,2,1,0:T(8,128)(2,1)}, bf16[1,2,768,1536]{3,2,1,0:T(8,128)(2,1)}, bf16[1,2,1536,768]{3,2,1,0:T(8,128)(2,1)}) async-done(((bf16[1,2,768,3,384]{2,4,3,1,0:T(8,128)(2,1)}, bf16[1,2,384,768]{3,2,1,0:T(8,128)(2,1)}, bf16[1,2,768,1536]{3,2,1,0:T(8,128)(2,1)}, bf16[1,2,1536,768]{3,2,1,0:T(8,128)(2,1)}), ...) | async-done | bytes 14155792 | tf_op jit(solution)/shard_map/psum | solution.py:303
  1274.6 7.9 broadcast_in_dim.562
  (816 shorter events, 542.0 us)
Async XLA Ops:
  7.2 14.7 %all-gather.3.cloned.1.call-start = ((), (), s32[]{:S(2)}) async-start(), calls=%async_computation | async-start | bytes 2211840 | tf_op jit(solution)/shard_map/all_gather | solution.py:209
  7.9 60.0 %all-reduce.20.cloned.1.call-start = ((), (), s32[]{:S(2)}) async-start(), calls=%async_computation.1 | async-start | bytes 2949120 | tf_op jit(solution)/shard_map/psum | solution.py:91
  14.2 333.4 %copy-start.6 = (bf16[1,1,768,3,384]{2,4,3,1,0:T(8,128)(2,1)}, bf16[1,1,768,3,384]{2,4,3,1,0:T(8,128)(2,1)S(1)}, u32[]{:S(2)}) copy-start(bf16[1,1,768,3,384]{2,4,3,1,0:T(8,128)(2,1)S(1)} %copy.232) | copy-start | bytes 5308420
  17.7 117.4 %copy-start.178 = (pred[480]{0:T(512)(128)(4,1)}, pred[480]{0:T(512)(128)(4,1)S(1)}, u32[]{:S(2)}) copy-start(pred[480]{0:T(512)(128)(4,1)S(1)} %get-tuple-element.71) | copy-start | bytes 1444
  46.3 61.8 %all-reduce.22.cloned.1.call-start = ((), (), s32[]{:S(2)}) async-start(), calls=%async_computation.2 | async-start | bytes 1474560 | tf_op jit(solution)/shard_map/psum | solution.py:100
  46.6 179.5 %copy-start.119 = (f32[768]{0:T(1024)}, f32[768]{0:T(1024)S(1)}, u32[]{:S(2)}) copy-start(f32[768]{0:T(1024)S(1)} %get-tuple-element.61) | copy-start | bytes 9220
  87.6 96.4 %all-reduce.24.cloned.1.call-start = ((), (), s32[]{:S(2)}) async-start(), calls=%async_computation.3 | async-start | bytes 2949120 | tf_op jit(solution)/shard_map/psum | solution.py:91
  113.3 20.1 %collective-permute-start = (bf16[480,768]{1,0:T(8,128)(2,1)}, bf16[480,768]{1,0:T(8,128)(2,1)}, u32[]{:S(2)}, u32[]{:S(2)}) collective-permute-start(bf16[480,768]{1,0:T(8,128)(2,1)} %get-tuple-element.128), channel_id=1, source_target_pairs={{0,16},{1,17},{2,18},{3,19},{4,20},{5,21},{6,22},{7,23},{8,24},{9,... | collective-permute-start | bytes 2211848 | tf_op jit(solution)/shard_map/ppermute | solution.py:19
  160.6 62.7 %all-reduce.26.cloned.1.call-start = ((), (), s32[]{:S(2)}) async-start(), calls=%async_computation.4 | async-start | bytes 1474560 | tf_op jit(solution)/shard_map/psum | solution.py:100
  202.8 201.1 %all-reduce.36.cloned.1.call-start = ((), (), s32[]{:S(2)}) async-start(), calls=%async_computation.10 | async-start | bytes 11796480 | tf_op jit(solution)/shard_map/psum | solution.py:91
  228.6 20.1 %collective-permute-start.1 = (bf16[480,768]{1,0:T(8,128)(2,1)}, bf16[480,768]{1,0:T(8,128)(2,1)}, u32[]{:S(2)}, u32[]{:S(2)}) collective-permute-start(bf16[480,768]{1,0:T(8,128)(2,1)} %get-tuple-element.124), channel_id=1, source_target_pairs={{0,16},{1,17},{2,18},{3,19},{4,20},{5,21},{6,22},{7,23},{8,24},{9,... | collective-permute-start | bytes 2211848 | tf_op jit(solution)/shard_map/ppermute | solution.py:19
  370.2 72.6 %all-reduce.28.cloned.1.call-start = ((), (), s32[]{:S(2)}) async-start(), calls=%async_computation.6 | async-start | bytes 1474560 | tf_op jit(solution)/shard_map/psum | solution.py:100
  422.3 32.9 %all-gather.5.cloned.1.call-start = ((), (), s32[]{:S(2)}) async-start(), calls=%async_computation.5 | async-start | bytes 2211840 | tf_op jit(solution)/shard_map/all_gather | solution.py:210
  423.1 85.4 %all-reduce.30.cloned.1.call-start = ((), (), s32[]{:S(2)}) async-start(), calls=%async_computation.7 | async-start | bytes 1474560 | tf_op jit(solution)/shard_map/psum | solution.py:149
  488.0 73.3 %all-reduce.44.cloned.1.call-start = ((), (), s32[]{:S(2)}) async-start(), calls=%async_computation.14 | async-start | bytes 2949120 | tf_op jit(solution)/shard_map/psum | solution.py:100
  539.6 89.5 %all-reduce.32.cloned.1.call-start = ((), (), s32[]{:S(2)}) async-start(), calls=%async_computation.8 | async-start | bytes 1474560 | tf_op jit(solution)/shard_map/psum | solution.py:149
  577.1 20.5 %collective-permute-start.2 = (bf16[480,768]{1,0:T(8,128)(2,1)S(1)}, bf16[480,768]{1,0:T(8,128)(2,1)S(1)}, u32[]{:S(2)}, u32[]{:S(2)}) collective-permute-start(bf16[480,768]{1,0:T(8,128)(2,1)S(1)} %fusion.273), channel_id=1, source_target_pairs={{16,0},{17,1},{18,2},{19,3},{20,4},{21,5},{22,6},{23,7},{24,8},{25... | collective-permute-start | bytes 2211848 | tf_op jit(solution)/shard_map/ppermute | solution.py:19
  609.5 68.3 %all-reduce.42.cloned.1.call-start = ((), (), s32[]{:S(2)}) async-start(), calls=%async_computation.13 | async-start | bytes 2949120 | tf_op jit(solution)/shard_map/psum | solution.py:100
  656.1 110.7 %all-reduce.34.cloned.1.call-start = ((), (), s32[]{:S(2)}) async-start(), calls=%async_computation.9 | async-start | bytes 1474560 | tf_op jit(solution)/shard_map/psum | solution.py:149
  694.4 20.5 %collective-permute-start.3 = (bf16[480,768]{1,0:T(8,128)(2,1)S(1)}, bf16[480,768]{1,0:T(8,128)(2,1)S(1)}, u32[]{:S(2)}, u32[]{:S(2)}) collective-permute-start(bf16[480,768]{1,0:T(8,128)(2,1)S(1)} %fusion.274), channel_id=1, source_target_pairs={{16,0},{17,1},{18,2},{19,3},{20,4},{21,5},{22,6},{23,7},{24,8},{25... | collective-permute-start | bytes 2211848 | tf_op jit(solution)/shard_map/ppermute | solution.py:19
  741.6 126.1 %all-reduce.40.cloned.1.call-start = ((), (), s32[]{:S(2)}) async-start(), calls=%async_computation.12 | async-start | bytes 2949120 | tf_op jit(solution)/shard_map/psum | solution.py:100
  798.1 468.3 %all-reduce.38.cloned.1.call-start = ((), (), s32[]{:S(2)}) async-start(), calls=%async_computation.11 | async-start | bytes 28311552 | tf_op jit(solution)/shard_map/psum | solution.py:303
  822.2 45.5 %copy-start.9 = (f32[480,768]{1,0:T(8,128)S(1)}, f32[480,768]{1,0:T(8,128)}, u32[]{:S(2)}) copy-start(f32[480,768]{1,0:T(8,128)} %get-tuple-element.76) | copy-start | bytes 4423684
  822.2 45.5 %copy-start.16 = (bf16[480,768]{1,0:T(8,128)(2,1)S(1)}, bf16[480,768]{1,0:T(8,128)(2,1)}, u32[]{:S(2)}) copy-start(bf16[480,768]{1,0:T(8,128)(2,1)} %get-tuple-element.120) | copy-start | bytes 2211844
  (221 other events, 976.3 us)
Sparse Core Ops, SparseCore 0:
  9.6 12.3 all-gather.2
  46.4 21.4 all-reduce.19
  87.8 20.2 all-reduce.21
  160.7 23.2 all-reduce.23
  203.0 20.2 all-reduce.25
  370.3 33.6 all-reduce.35
  422.4 20.2 all-reduce.27
  444.4 10.7 all-gather.4
  488.1 20.2 all-reduce.29
  539.7 21.5 all-reduce.43
  609.6 19.4 all-reduce.31
  656.2 21.5 all-reduce.41
  741.7 19.4 all-reduce.33
  798.3 20.6 all-reduce.39
  824.8 441.6 all-reduce.37
where the time goes:
time: 1300 us; the launch traced here: 1290 us
  waiting for transfers between devices  617 us (47%)
  matrix products  284 us (22%)
  local copies, waits for them, and re-layouts  189 us (15%)
  other arithmetic  133 us (10%)
  blocking collectives  39.9 us (3%)
  between operations  17.1 us (1%)
  starting transfers between devices  14.5 us (1%)
    psum x1, waiting for transfers between devices, shards(): lax.psum(mixer_totals[0].astype(jnp.bfloat16), 'dp').astype(jnp.float32)  389 us
    dot_general x24, matrix products, pick_product(): first_set = jnp.dot(rows, weights[0], preferred_element_type=jnp.float32)  85.8 us
    psum x3, waiting for transfers between devices, layer_forward(): attn_total = lax.psum(pick_product(mixed_heads, output, is_light), 'tensor')  78.1 us
    unnamed x473, local copies, waits for them, and re-layouts  72 us
    ppermute x4, waiting for transfers between devices, from_behind(): lax.ppermute(value, axis, [(source, source + steps) for source in range(l...  62.2 us
    psum x6, waiting for transfers between devices, layer_forward(): lax.psum(pick_product(hidden, down_w, is_light).astype(jnp.bfloat16), 'te...  56.5 us
    dot_general x24, matrix products, pick_product(): second_set = jnp.dot(rows, weights[1], preferred_element_type=jnp.float32)  51.7 us
    psum x1, blocking collectives, shards(): lax.psum(feed_totals[2].astype(jnp.bfloat16), 'dp').astype(jnp.float32)  39.9 us
  transfers between devices with their start and end apart: 19, of which 17 were waited for; matrix products, arithmetic and copies ran while one was open for 11% of the time, Pallas kernels for 0%

commit v1 on v0

v1 whole, which is shorter than its diff:
```python
import jax
import jax.numpy as jnp
from jax import lax
from jax.sharding import PartitionSpec as P

HEAD_DIM = 64
SYMBOLS = 24
SEQ = 160
PARTS = 2

root_half = 0.7071067811865476
root_two_pi = 0.3989422804014327
BF = jnp.bfloat16
F32 = jnp.float32


def swap(value):
    return lax.ppermute(value, "tensor", [(0, 1), (1, 0)])


def pick_product(rows, weights, is_light):
    first_set = jnp.dot(rows, weights[0], preferred_element_type=F32)
    second_set = jnp.dot(rows, weights[1], preferred_element_type=F32)
    return jnp.where(is_light, second_set, first_set)


def back_product(grads, weights, is_light):
    contract_cols = (((1,), (1,)), ((), ()))
    first_set = lax.dot_general(grads, weights[0], contract_cols, preferred_element_type=F32)
    second_set = lax.dot_general(grads, weights[1], contract_cols, preferred_element_type=F32)
    return jnp.where(is_light, second_set, first_set)


def weight_pair(rows, grads, is_light):
    contract_rows = (((0,), (0,)), ((), ()))
    zero_rows = jnp.zeros_like(rows)
    heavy_rows = jnp.where(is_light, zero_rows, rows)
    light_rows = jnp.where(is_light, rows, zero_rows)
    first_set = lax.dot_general(heavy_rows, grads, contract_rows, preferred_element_type=F32)
    second_set = lax.dot_general(light_rows, grads, contract_rows, preferred_element_type=F32)
    return [first_set.astype(BF), second_set.astype(BF)]


def layer_norm(rows, gain, shift):
    centred = rows - jnp.mean(rows, axis=-1, keepdims=True)
    inv_root = lax.rsqrt(jnp.mean(centred * centred, axis=-1, keepdims=True) + 1e-05)
    normal = centred * inv_root
    return (normal * gain + shift, normal, inv_root)


def norm_back(grads, normal, inv_root, gain):
    scaled = grads * gain
    inner = (
        scaled
        - jnp.mean(scaled, axis=-1, keepdims=True)
        - normal * jnp.mean(scaled * normal, axis=-1, keepdims=True)
    )
    return inner * inv_root


def attn_forward(rows_in, is_light, key_live, params):
    joint, output = params[:2]
    chains = key_live.shape[0]
    local_heads = output.shape[1] // HEAD_DIM
    joined = pick_product(rows_in, joint, is_light).astype(BF)
    pieces = joined.reshape(chains, SEQ, 3, local_heads, HEAD_DIM)
    q, k, v = pieces[:, :, 0], pieces[:, :, 1], pieces[:, :, 2]
    raw_scores = jnp.einsum("cqhd,ckhd->chqk", q, k, preferred_element_type=F32)
    scores = jnp.where(key_live[:, None, None, :], raw_scores * HEAD_DIM ** (-0.5), -1000000000.0)
    shifted = jnp.exp(scores - jnp.max(scores, axis=-1, keepdims=True))
    probs = shifted / jnp.sum(shifted, axis=-1, keepdims=True)
    mixed = jnp.einsum("chqk,ckhd->cqhd", probs.astype(BF), v, preferred_element_type=F32)
    mixed = mixed.astype(BF).reshape(rows_in.shape[0], -1)
    part = pick_product(mixed, output, is_light).astype(BF)
    return part, (q, k, v, probs, mixed)


def feed_forward(rows_in, part, other, is_light, params):
    joint, output, up_w, up_b, down_w, gains, shifts = params
    attn = part.astype(F32) + other.astype(F32)
    first, normal_one, root_one = layer_norm(rows_in.astype(F32) + attn, gains[0], shifts[0])
    first_low = first.astype(BF)
    pre = pick_product(first_low, up_w, is_light) + jnp.where(is_light, up_b[1], up_b[0]).astype(F32)
    hidden = jax.nn.gelu(pre, approximate=False).astype(BF)
    down = pick_product(hidden, down_w, is_light).astype(BF)
    return down, (first, normal_one, root_one, first_low, pre, hidden)


def last_norm(first, down, other, params):
    gains, shifts = params[5:]
    return layer_norm(first + (down.astype(F32) + other.astype(F32)), gains[1], shifts[1])


def feed_back(grad, normal_two, root_two, kept, is_light, params):
    joint, output, up_w, up_b, down_w, gains, shifts = params
    first, normal_one, root_one, first_low, pre, hidden = kept
    dr2 = norm_back(grad, normal_two, root_two, gains[1])
    d_down = dr2.astype(BF)
    d_hidden = back_product(d_down, down_w, is_light)
    slope = 0.5 * (1.0 + lax.erf(pre * root_half)) + pre * jnp.exp(-0.5 * pre * pre) * root_two_pi
    d_pre = (d_hidden * slope).astype(BF)
    part = back_product(d_pre, up_w, is_light).astype(BF)
    return dr2, d_down, d_pre, part


def attn_back(dr2, part, other, feed_kept, attn_kept, is_light, params):
    joint, output, up_w, up_b, down_w, gains, shifts = params
    first, normal_one, root_one, first_low, pre, hidden = feed_kept
    q, k, v, probs, mixed = attn_kept
    d_first = dr2 + (part.astype(F32) + other.astype(F32))
    dr1 = norm_back(d_first, normal_one, root_one, gains[0])
    d_attn = dr1.astype(BF)
    d_mixed = back_product(d_attn, output, is_light).astype(BF).reshape(q.shape)
    d_probs = jnp.einsum("cqhd,ckhd->chqk", d_mixed, v, preferred_element_type=F32)
    d_scores = (
        probs * (d_probs - jnp.sum(probs * d_probs, axis=-1, keepdims=True))
    ).astype(BF)
    scale = HEAD_DIM ** (-0.5)
    dq = jnp.einsum("chqk,ckhd->cqhd", d_scores, k, preferred_element_type=F32) * scale
    dk = jnp.einsum("chqk,cqhd->ckhd", d_scores, q, preferred_element_type=F32) * scale
    dv = jnp.einsum("chqk,cqhd->ckhd", probs.astype(BF), d_mixed, preferred_element_type=F32)
    d_joined = jnp.stack([dq, dk, dv], axis=2).astype(BF).reshape(dr1.shape[0], -1)
    d_rows = back_product(d_joined, joint, is_light).astype(BF)
    return d_first, dr1, d_attn, d_joined, d_rows


def ring_order(count):
    return list(range(0, count, 2)) + list(range(1, count, 2))[::-1]


def ring_sum(heavy, light):
    count = lax.axis_size("dp")
    order = ring_order(count)
    rank = lax.axis_index("dp")
    place = jnp.zeros((), jnp.int32)
    for at, member in enumerate(order):
        place = jnp.where(rank == member, at, place)
    ahead = [(order[i], order[(i + 1) % count]) for i in range(count)]
    behind = [(b, a) for a, b in ahead]
    shape = heavy.shape
    rows = shape[0] // count

    def shard(whole, index):
        return lax.dynamic_slice_in_dim(whole, lax.rem(index, count) * rows, rows, 0)

    results = []
    for whole, pairs, sign in ((heavy, ahead, -1), (light, behind, 1)):
        moving = shard(whole, place + sign + count)
        for step in range(count - 1):
            moving = lax.ppermute(moving, "dp", pairs)
            index = place + sign * (step + 2) + 2 * count
            moving = (moving.astype(F32) + shard(whole, index).astype(F32)).astype(BF)
        out = jnp.zeros(shape, F32)
        index = place
        for step in range(count):
            out = lax.dynamic_update_slice_in_dim(
                out, moving.astype(F32), lax.rem(index, count) * rows, 0
            )
            if step < count - 1:
                moving = lax.ppermute(moving, "dp", pairs)
                index = place + sign * (step + 1) + count
        results.append(out)
    return jnp.stack(results)


def shards(
    chain_inputs,
    cotangent,
    chain_tags,
    pad_mask,
    predicted,
    target_ids,
    joint_proj,
    output_proj,
    up_proj,
    up_bias,
    down_proj,
    norm_gain,
    norm_shift,
):
    section = lax.axis_index("section")
    core = lax.axis_index("tensor")
    tokens, half = chain_inputs.shape
    width = 2 * half

    def side_by_side(own, other):
        return jnp.where(
            core == 0,
            jnp.concatenate([own, other], axis=1),
            jnp.concatenate([other, own], axis=1),
        )

    def own_half(value):
        return lax.dynamic_slice_in_dim(value, core * half, half, 1)

    rows_all = side_by_side(chain_inputs, swap(chain_inputs))
    cot_all = side_by_side(cotangent, swap(cotangent))
    size = tokens // PARTS
    joint = joint_proj[0].reshape(2, width, -1)
    params = (
        joint,
        output_proj[0],
        up_proj[0],
        up_bias[0],
        down_proj[0],
        norm_gain[0],
        norm_shift[0],
    )
    light_all = (jnp.repeat(chain_tags, SEQ) > 0)[:, None]
    live_all = (pad_mask > 0).reshape(-1, SEQ)
    spans = [slice(p * size, (p + 1) * size) for p in range(PARTS)]
    lights = [light_all[s] for s in spans]
    lives = [live_all[s.start // SEQ : s.stop // SEQ] for s in spans]
    own_rows = [rows_all[s] for s in spans]
    own_cot = [cot_all[s] for s in spans]

    def forward(rows, p):
        part, attn_kept = attn_forward(rows, lights[p], lives[p], params)
        down, feed_kept = feed_forward(rows, part, swap(part), lights[p], params)
        result, normal, root = last_norm(feed_kept[0], down, swap(down), params)
        return result.astype(BF), attn_kept, feed_kept, normal, root

    def backward(grad, kept, p):
        low, attn_kept, feed_kept, normal, root = kept
        dr2, d_down, d_pre, part = feed_back(grad, normal, root, feed_kept, lights[p], params)
        d_first, dr1, d_attn, d_joined, d_rows = attn_back(
            dr2, part, swap(part), feed_kept, attn_kept, lights[p], params
        )
        return d_down, d_pre, d_first, dr1, d_attn, d_joined, d_rows

    def to_section(value, pairs):
        moved = lax.ppermute(own_half(value), "section", pairs)
        return side_by_side(moved, swap(moved))

    arrived = []
    for p in range(PARTS):
        low = forward(own_rows[p], p)[0]
        arrived.append(to_section(low, [(0, 1)]))
    rows_in = [jnp.where(section == 0, own_rows[p], arrived[p]) for p in range(PARTS)]
    kept = [forward(rows_in[p], p) for p in range(PARTS)]
    grads_in = []
    for p in range(PARTS):
        d_down, d_pre, d_first, dr1, d_attn, d_joined, d_rows = backward(
            own_cot[p].astype(F32), kept[p], p
        )
        own = own_half(d_rows)
        total = own_half(dr1) + (own.astype(F32) + swap_other(d_rows, core, half).astype(F32))
        moved = lax.ppermute(total.astype(BF), "section", [(1, 0)])
        back = side_by_side(moved, swap(moved))
        grads_in.append(jnp.where(section == 1, own_cot[p], back).astype(F32))
    outs = [backward(grads_in[p], kept[p], p) for p in range(PARTS)]

    def whole(pieces):
        return jnp.concatenate(pieces, axis=0)

    d_down = whole([o[0] for o in outs])
    d_pre = whole([o[1] for o in outs])
    d_first = whole([o[2] for o in outs])
    d_attn = whole([o[4] for o in outs])
    d_joined = whole([o[5] for o in outs])
    hidden = whole([k[2][5] for k in kept])
    first_low = whole([k[2][3] for k in kept])
    mixed = whole([k[1][4] for k in kept])
    rows_whole = whole(rows_in)
    normal_one = whole([k[2][1] for k in kept])
    normal_two = whole([k[3] for k in kept])
    grad_whole = whole(grads_in)

    down_sum = ring_sum(*weight_pair(hidden, d_down, light_all))
    up_sum = ring_sum(*weight_pair(first_low, d_pre, light_all))
    output_sum = ring_sum(*weight_pair(mixed, d_attn, light_all))
    pair = weight_pair(rows_whole, d_joined, light_all)
    pair = [g.reshape(width, 3, half).transpose(1, 0, 2).reshape(3 * width, half) for g in pair]
    joint_sum = ring_sum(*pair).reshape(2, 3, width, half).transpose(0, 2, 1, 3)

    input_pieces = []
    for p in range(PARTS):
        d_rows, dr1 = outs[p][6], outs[p][3]
        input_pieces.append(
            own_half(dr1)
            + (own_half(d_rows).astype(F32) + swap_other(d_rows, core, half).astype(F32))
        )
    input_grads = whole(input_pieces)[None]
    layer_outputs = own_half(whole([k[0] for k in kept]))[None]

    pre_wide = d_pre.astype(F32)
    zero = jnp.zeros_like(pre_wide)
    bias = jnp.stack(
        [
            jnp.sum(jnp.where(light_all, zero, pre_wide), 0),
            jnp.sum(jnp.where(light_all, pre_wide, zero), 0),
        ]
    )
    gain = jnp.stack([jnp.sum(d_first * normal_one, 0), jnp.sum(grad_whole * normal_two, 0)])
    shift = jnp.stack([jnp.sum(d_first, 0), jnp.sum(grad_whole, 0)])
    symbols = jnp.arange(SYMBOLS, dtype=jnp.int32)
    target_hits = (target_ids[:, None] == symbols[None, :]) & (pad_mask[:, None] > 0)
    correct_hits = target_hits & (predicted == target_ids)[:, None]
    counts = jnp.stack([jnp.sum(target_hits, 0), jnp.sum(correct_hits, 0)]).astype(F32)
    small = [bias, gain, shift, counts]
    packed = jnp.concatenate([s.reshape(-1) for s in small])
    packed = lax.psum(packed, "dp")
    results = []
    start = 0
    for s in small:
        results.append(packed[start : start + s.size].reshape(s.shape))
        start += s.size
    bias, gain, shift, counts = results
    return (
        layer_outputs,
        input_grads,
        joint_sum[None],
        output_sum[None],
        up_sum[None],
        bias[None],
        down_sum[None],
        gain[None],
        shift[None],
        counts.astype(jnp.int32),
    )


def swap_other(value, core, half):
    theirs = lax.dynamic_slice_in_dim(value, (1 - core) * half, half, 1)
    return swap(theirs)


def solution(mesh):
    return jax.shard_map(
        shards,
        mesh=mesh,
        in_specs=(
            P("dp", "tensor"),
            P("dp", "tensor"),
            P("dp"),
            P("dp"),
            P("dp"),
            P("dp"),
            P("section", None, None, None, "tensor"),
            P("section", None, "tensor", None),
            P("section", None, None, "tensor"),
            P("section", None, "tensor"),
            P("section", None, "tensor", None),
            P("section", None, None),
            P("section", None, None),
        ),
        out_specs=(
            P("section", "dp", "tensor"),
            P("section", "dp", "tensor"),
            P("section", None, None, None, "tensor"),
            P("section", None, "tensor", None),
            P("section", None, None, "tensor"),
            P("section", None, "tensor"),
            P("section", None, "tensor", None),
            P("section", None, None),
            P("section", None, None),
            P(),
        ),
        check_vma=False,
    )
```

time: 1300 us -> 887 us (0.68)
  waiting for transfers between devices: 617 us -> 213 us
  starting transfers between devices: 14.5 us -> 132 us
  matrix products: 284 us -> 207 us
  other arithmetic: 133 us -> 107 us
  local copies, waits for them, and re-layouts: 189 us -> 174 us
    psum x13 -> x0, waiting for transfers between devices: 541 us -> none  [the longest x1 389 us: shards(): lax.psum(mixer_totals[0].astype(jnp.bfloat16), 'dp').astype(jnp.float32)]
    ppermute x4 -> x138, waiting for transfers between devices: 62.2 us -> 213 us  [the longest x112 170 us: ring_sum(): moving = lax.ppermute(moving, 'dp', pairs)]
    ppermute x4 -> x138, starting transfers between devices: 12.4 us -> 132 us  [the longest x112 118 us: ring_sum(): moving = lax.ppermute(moving, 'dp', pairs)]
    dot_general x72 -> x56, matrix products: 163 us -> 125 us  [the longest x16 62.8 us: pick_product(): first_set = jnp.dot(rows, weights[0], preferred_element_type=F32)]
    unnamed x473 -> x426, local copies, waits for them, and re-layouts: 72 us -> 45.2 us
    dot_general x12 -> x4, matrix products: 38.4 us -> 12.4 us  [weight_pair(): lax.dot_general(heavy_rows, grads, contract_rows, preferred_element_type=...]
    dot_general x12 -> x4, matrix products: 38.7 us -> 13.1 us  [weight_pair(): lax.dot_general(light_rows, grads, contract_rows, preferred_element_type=...]
    broadcast_in_dim x2 -> x1, other arithmetic: 20.7 us -> 4.59 us  [shards(): up_sum[None]]
  transfers between devices with their start and end apart: 19 -> 138, of which waited for: 17 -> 69; matrix products, arithmetic and copies ran while one was open for 11% -> 35% of each run, Pallas kernels for 0% -> 0%
where the time goes in v1:
time: 887 us; the launch traced here: 875 us
  waiting for transfers between devices  213 us (24%)
  matrix products  207 us (23%)
  local copies, waits for them, and re-layouts  174 us (20%)
  starting transfers between devices  132 us (15%)
  other arithmetic  107 us (12%)
  blocking collectives  36.8 us (4%)
    ppermute x112, waiting for transfers between devices, ring_sum(): moving = lax.ppermute(moving, 'dp', pairs)  170 us
    ppermute x112, starting transfers between devices, ring_sum(): moving = lax.ppermute(moving, 'dp', pairs)  118 us
    dot_general x16, matrix products, pick_product(): first_set = jnp.dot(rows, weights[0], preferred_element_type=F32)  62.8 us
    unnamed x426, local copies, waits for them, and re-layouts  45.2 us
    psum x1, blocking collectives, shards(): packed = lax.psum(packed, 'dp')  36.8 us
    dot_general x16, matrix products, back_product(): lax.dot_general(grads, weights[1], contract_cols, preferred_element_type=...  33.3 us
    dot_general x16, matrix products, pick_product(): second_set = jnp.dot(rows, weights[1], preferred_element_type=F32)  28.2 us
    convert_element_type x6, local copies, waits for them, and re-layouts, attn_back(): jnp.stack([dq, dk, dv], axis=2).astype(BF).reshape(dr1.shape[0], -1)  27.7 us
  transfers between devices with their start and end apart: 138, of which 69 were waited for; matrix products, arithmetic and copies ran while one was open for 35% of the time, Pallas kernels for 0%

profile of v1, /device:TPU:0, one launch (start us, length us, event | category | flops | bytes accessed | tf_op | source)
XLA Modules:
  0.0 874.9 jit_solution(632005362663898295)
XLA Ops:
  73.2 7.7 fusion.12
  80.9 11.2 %fusion.82 = bf16[480,768]{1,0:T(8,128)(2,1)S(1)} fusion(bf16[480,1536]{1,0:T(8,128)(2,1)S(1)} %fusion.12, bf16[1,2,1536,768]{3,2,1,0:T(8,128)(2,1)S(1)} %bitcast.603), kind=kOutput, calls=%fused_computation.173 | convolution fusion | flops 1132462080 | bytes 4571136 | tf_op jit(solution)/shard_map/dot_general | solution.py:22
  103.0 9.1 %fusion.18 = bf16[480,1536]{1,0:T(8,128)(2,1)S(1)} fusion(f32[480,1536]{1,0:T(8,128)S(1)} %fusion.122, bf16[480,768]{1,0:T(8,128)(2,1)S(1)} %get-tuple-element.113, pred[480]{0:T(512)(128)(4,1)S(1)} %copy-done.161, bf16[1536]{0:T(1024)(128)(2,1)S(1)} %get-tuple-element.41, bf16[1536]{0:T(1024)(128)(2,1)S(1)} %get-tuple-element.40, ...), kind=kOutput, calls=%fused_computation.53 | convolution fusion | flops 1183334400 | bytes 7526880 | tf_op jit(solution)/shard_map/dot_general | solution.py:22
  124.6 7.6 collective-permute-done.3
  132.2 7.1 collective-permute-done.9
  210.1 7.6 fusion.15
  225.1 7.6 fusion.21
  258.0 5.8 fusion.381
  297.5 5.5 convert_element_type.1105
  312.2 5.3 convert_element_type.1077
  326.3 10.6 %collective-permute-done.22 = bf16[480,384]{1,0:T(8,128)(2,1)} collective-permute-done((bf16[480,384]{1,0:T(8,128)(2,1)S(1)}, bf16[480,384]{1,0:T(8,128)(2,1)}, u32[]{:S(2)}, u32[]{:S(2)}) %collective-permute-start.22) | collective-permute-done | bytes 368672 | tf_op jit(solution)/shard_map/ppermute | solution.py:248
  337.0 7.3 collective-permute-done.16
  469.9 5.4 convert_element_type.1120
  482.7 5.5 convert_element_type.1092
  492.3 5.7 convolution_convert_fusion.4
  507.9 36.8 %psum.7 = f32[6192]{0:T(1024)S(1)} all-reduce(f32[6192]{0:T(1024)S(1)} %pad_maximum_fusion.25), channel_id=1, replica_groups=mesh['section'=2,'dp'=8,'tensor'=2] {'dp'}, use_global_device_ids=true, to_apply=%region_54.55 | all-reduce | flops 6192 | bytes 49536 | tf_op jit(solution)/shard_map/psum | solution.py:302
  590.3 6.6 collective-permute-done.70
  654.4 5.6 collective-permute-done.42
  696.4 9.1 %collective-permute-done.79 = bf16[48,768]{1,0:T(8,128)(2,1)S(1)} collective-permute-done((bf16[48,768]{1,0:T(8,128)(2,1)S(1)}, bf16[48,768]{1,0:T(8,128)(2,1)S(1)}, u32[]{:S(2)}, u32[]{:S(2)}) %collective-permute-start.79) | collective-permute-done | bytes 73760 | tf_op jit(solution)/shard_map/ppermute | solution.py:160
  710.8 5.2 collective-permute-done.80
  748.8 14.7 %collective-permute-done.46 = bf16[288,384]{1,0:T(8,128)(2,1)S(1)} collective-permute-done((bf16[288,384]{1,0:T(8,128)(2,1)S(1)}, bf16[288,384]{1,0:T(8,128)(2,1)S(1)}, u32[]{:S(2)}, u32[]{:S(2)}) %collective-permute-start.46) | collective-permute-done | bytes 221216 | tf_op jit(solution)/shard_map/ppermute | solution.py:150
  765.8 5.9 collective-permute-done.32
  812.5 12.7 %collective-permute-done.50 = bf16[288,384]{1,0:T(8,128)(2,1)S(1)} collective-permute-done((bf16[288,384]{1,0:T(8,128)(2,1)S(1)}, bf16[288,384]{1,0:T(8,128)(2,1)S(1)}, u32[]{:S(2)}, u32[]{:S(2)}) %collective-permute-start.50) | collective-permute-done | bytes 221216 | tf_op jit(solution)/shard_map/ppermute | solution.py:160
  867.8 6.7 maximum_bitcast_fusion.1
  (1079 shorter events, 657.6 us)
Async XLA Ops:
  139.3 97.0 %collective-permute-start.13 = (bf16[960,384]{1,0:T(8,128)(2,1)}, bf16[960,384]{1,0:T(8,128)(2,1)}, u32[]{:S(2)}, u32[]{:S(2)}) collective-permute-start(bf16[960,384]{1,0:T(8,128)(2,1)} %param.14), channel_id=1, source_target_pairs={{0,1},{1,0},{2,3},{3,2},{4,5},{5,4},{6,7},{7,6},{8,9},{9,8},{10,11... | collective-permute-start | bytes 2211848 | tf_op jit(solution)/shard_map/ppermute | solution.py:18
  387.7 41.3 %collective-permute-start.18 = (bf16[480,768]{1,0:T(8,128)(2,1)}, bf16[480,768]{1,0:T(8,128)(2,1)}, u32[]{:S(2)}, u32[]{:S(2)}) collective-permute-start(bf16[480,768]{1,0:T(8,128)(2,1)} %select_convert_fusion.5), channel_id=1, source_target_pairs={{0,1},{1,0},{2,3},{3,2},{4,5},{5,4},{6,7},{7,6},{8,9},{9,8},{10,11... | collective-permute-start | bytes 2211848 | tf_op jit(solution)/shard_map/ppermute | solution.py:18
  390.4 39.1 %collective-permute-start.24 = (bf16[480,768]{1,0:T(8,128)(2,1)}, bf16[480,768]{1,0:T(8,128)(2,1)}, u32[]{:S(2)}, u32[]{:S(2)}) collective-permute-start(bf16[480,768]{1,0:T(8,128)(2,1)} %select_convert_fusion.1), channel_id=1, source_target_pairs={{0,1},{1,0},{2,3},{3,2},{4,5},{5,4},{6,7},{7,6},{8,9},{9,8},{10,11... | collective-permute-start | bytes 2211848 | tf_op jit(solution)/shard_map/ppermute | solution.py:18
  419.1 153.4 %collective-permute-start.98 = (bf16[96,1536]{1,0:T(8,128)(2,1)}, bf16[96,1536]{1,0:T(8,128)(2,1)}, u32[]{:S(2)}, u32[]{:S(2)}) collective-permute-start(bf16[96,1536]{1,0:T(8,128)(2,1)} %add_convert_fusion.23), channel_id=1, source_target_pairs={{4,0},{8,4},{12,8},{14,12},{10,14},{6,10},{2,6},{0,2},{5,1},{9,5},... | collective-permute-start | bytes 884744 | tf_op jit(solution)/shard_map/ppermute | solution.py:150
  422.4 151.8 %collective-permute-start.84 = (bf16[96,1536]{1,0:T(8,128)(2,1)}, bf16[96,1536]{1,0:T(8,128)(2,1)}, u32[]{:S(2)}, u32[]{:S(2)}) collective-permute-start(bf16[96,1536]{1,0:T(8,128)(2,1)} %add_convert_fusion.30), channel_id=1, source_target_pairs={{0,4},{4,8},{8,12},{12,14},{14,10},{10,6},{6,2},{2,0},{1,5},{5,9},... | collective-permute-start | bytes 884744 | tf_op jit(solution)/shard_map/ppermute | solution.py:150
  425.5 150.0 %collective-permute-start.126 = (bf16[192,768]{1,0:T(8,128)(2,1)}, bf16[192,768]{1,0:T(8,128)(2,1)}, u32[]{:S(2)}, u32[]{:S(2)}) collective-permute-start(bf16[192,768]{1,0:T(8,128)(2,1)} %add_convert_fusion.9), channel_id=1, source_target_pairs={{4,0},{8,4},{12,8},{14,12},{10,14},{6,10},{2,6},{0,2},{5,1},{9,5},... | collective-permute-start | bytes 884744 | tf_op jit(solution)/shard_map/ppermute | solution.py:150
  429.0 149.6 %collective-permute-start.112 = (bf16[192,768]{1,0:T(8,128)(2,1)}, bf16[192,768]{1,0:T(8,128)(2,1)}, u32[]{:S(2)}, u32[]{:S(2)}) collective-permute-start(bf16[192,768]{1,0:T(8,128)(2,1)} %add_convert_fusion.16), channel_id=1, source_target_pairs={{0,4},{4,8},{8,12},{12,14},{14,10},{10,6},{6,2},{2,0},{1,5},{5,9},... | collective-permute-start | bytes 884744 | tf_op jit(solution)/shard_map/ppermute | solution.py:150
  572.5 38.6 %collective-permute-start.25 = (bf16[480,384]{1,0:T(8,128)(2,1)}, bf16[480,384]{1,0:T(8,128)(2,1)S(1)}, u32[]{:S(2)}, u32[]{:S(2)}) collective-permute-start(bf16[480,384]{1,0:T(8,128)(2,1)} %constant_dynamic-slice_fusion.8), channel_id=1, source_target_pairs={{0,1},{1,0},{2,3},{3,2},{4,5},{5,4},{6,7},{7,6},{8,9},{9,8},{10,11... | collective-permute-start | bytes 1105928 | tf_op jit(solution)/shard_map/ppermute | solution.py:18
  572.5 41.5 %collective-permute-start.19 = (bf16[480,384]{1,0:T(8,128)(2,1)}, bf16[480,384]{1,0:T(8,128)(2,1)S(1)}, u32[]{:S(2)}, u32[]{:S(2)}) collective-permute-start(bf16[480,384]{1,0:T(8,128)(2,1)} %constant_dynamic-slice_fusion.10), channel_id=1, source_target_pairs={{0,1},{1,0},{2,3},{3,2},{4,5},{5,4},{6,7},{7,6},{8,9},{9,8},{10,11... | collective-permute-start | bytes 1105928 | tf_op jit(solution)/shard_map/ppermute | solution.py:18
  587.9 37.4 %collective-permute-start.99 = (bf16[96,1536]{1,0:T(8,128)(2,1)S(1)}, bf16[96,1536]{1,0:T(8,128)(2,1)S(1)}, u32[]{:S(2)}, u32[]{:S(2)}) collective-permute-start(bf16[96,1536]{1,0:T(8,128)(2,1)S(1)} %add_convert_fusion.22), channel_id=1, source_target_pairs={{4,0},{8,4},{12,8},{14,12},{10,14},{6,10},{2,6},{0,2},{5,1},{9,5},... | collective-permute-start | bytes 884744 | tf_op jit(solution)/shard_map/ppermute | solution.py:150
  588.0 39.2 %collective-permute-start.85 = (bf16[96,1536]{1,0:T(8,128)(2,1)S(1)}, bf16[96,1536]{1,0:T(8,128)(2,1)S(1)}, u32[]{:S(2)}, u32[]{:S(2)}) collective-permute-start(bf16[96,1536]{1,0:T(8,128)(2,1)S(1)} %add_convert_fusion.29), channel_id=1, source_target_pairs={{0,4},{4,8},{8,12},{12,14},{14,10},{10,6},{6,2},{2,0},{1,5},{5,9},... | collective-permute-start | bytes 884744 | tf_op jit(solution)/shard_map/ppermute | solution.py:150
  629.5 46.4 %collective-permute-start.100 = (bf16[96,1536]{1,0:T(8,128)(2,1)S(1)}, bf16[96,1536]{1,0:T(8,128)(2,1)S(1)}, u32[]{:S(2)}, u32[]{:S(2)}) collective-permute-start(bf16[96,1536]{1,0:T(8,128)(2,1)S(1)} %add_convert_fusion.21), channel_id=1, source_target_pairs={{4,0},{8,4},{12,8},{14,12},{10,14},{6,10},{2,6},{0,2},{5,1},{9,5},... | collective-permute-start | bytes 884744 | tf_op jit(solution)/shard_map/ppermute | solution.py:150
  631.0 47.2 %collective-permute-start.86 = (bf16[96,1536]{1,0:T(8,128)(2,1)S(1)}, bf16[96,1536]{1,0:T(8,128)(2,1)S(1)}, u32[]{:S(2)}, u32[]{:S(2)}) collective-permute-start(bf16[96,1536]{1,0:T(8,128)(2,1)S(1)} %add_convert_fusion.28), channel_id=1, source_target_pairs={{0,4},{4,8},{8,12},{12,14},{14,10},{10,6},{6,2},{2,0},{1,5},{5,9},... | collective-permute-start | bytes 884744 | tf_op jit(solution)/shard_map/ppermute | solution.py:150
  633.4 44.9 %collective-permute-start.128 = (bf16[192,768]{1,0:T(8,128)(2,1)S(1)}, bf16[192,768]{1,0:T(8,128)(2,1)S(1)}, u32[]{:S(2)}, u32[]{:S(2)}) collective-permute-start(bf16[192,768]{1,0:T(8,128)(2,1)S(1)} %add_convert_fusion.7), channel_id=1, source_target_pairs={{4,0},{8,4},{12,8},{14,12},{10,14},{6,10},{2,6},{0,2},{5,1},{9,5},... | collective-permute-start | bytes 884744 | tf_op jit(solution)/shard_map/ppermute | solution.py:150
  633.7 46.8 %collective-permute-start.114 = (bf16[192,768]{1,0:T(8,128)(2,1)S(1)}, bf16[192,768]{1,0:T(8,128)(2,1)S(1)}, u32[]{:S(2)}, u32[]{:S(2)}) collective-permute-start(bf16[192,768]{1,0:T(8,128)(2,1)S(1)} %add_convert_fusion.14), channel_id=1, source_target_pairs={{0,4},{4,8},{8,12},{12,14},{14,10},{10,6},{6,2},{2,0},{1,5},{5,9},... | collective-permute-start | bytes 884744 | tf_op jit(solution)/shard_map/ppermute | solution.py:150
  680.5 42.0 %collective-permute-start.101 = (bf16[96,1536]{1,0:T(8,128)(2,1)S(1)}, bf16[96,1536]{1,0:T(8,128)(2,1)S(1)}, u32[]{:S(2)}, u32[]{:S(2)}) collective-permute-start(bf16[96,1536]{1,0:T(8,128)(2,1)S(1)} %add_convert_fusion.20), channel_id=1, source_target_pairs={{4,0},{8,4},{12,8},{14,12},{10,14},{6,10},{2,6},{0,2},{5,1},{9,5},... | collective-permute-start | bytes 884744 | tf_op jit(solution)/shard_map/ppermute | solution.py:150
  682.7 37.6 %collective-permute-start.87 = (bf16[96,1536]{1,0:T(8,128)(2,1)S(1)}, bf16[96,1536]{1,0:T(8,128)(2,1)S(1)}, u32[]{:S(2)}, u32[]{:S(2)}) collective-permute-start(bf16[96,1536]{1,0:T(8,128)(2,1)S(1)} %add_convert_fusion.27), channel_id=1, source_target_pairs={{0,4},{4,8},{8,12},{12,14},{14,10},{10,6},{6,2},{2,0},{1,5},{5,9},... | collective-permute-start | bytes 884744 | tf_op jit(solution)/shard_map/ppermute | solution.py:150
  694.1 31.0 %collective-permute-start.129 = (bf16[192,768]{1,0:T(8,128)(2,1)S(1)}, bf16[192,768]{1,0:T(8,128)(2,1)S(1)}, u32[]{:S(2)}, u32[]{:S(2)}) collective-permute-start(bf16[192,768]{1,0:T(8,128)(2,1)S(1)} %add_convert_fusion.6), channel_id=1, source_target_pairs={{4,0},{8,4},{12,8},{14,12},{10,14},{6,10},{2,6},{0,2},{5,1},{9,5},... | collective-permute-start | bytes 884744 | tf_op jit(solution)/shard_map/ppermute | solution.py:150
  738.1 34.0 %collective-permute-start.103 = (bf16[96,1536]{1,0:T(8,128)(2,1)S(1)}, bf16[96,1536]{1,0:T(8,128)(2,1)S(1)}, u32[]{:S(2)}, u32[]{:S(2)}) collective-permute-start(bf16[96,1536]{1,0:T(8,128)(2,1)S(1)} %get-tuple-element.61), channel_id=1, source_target_pairs={{4,0},{8,4},{12,8},{14,12},{10,14},{6,10},{2,6},{0,2},{5,1},{9,5},... | collective-permute-start | bytes 884744 | tf_op jit(solution)/shard_map/ppermute | solution.py:160
  741.4 32.8 %collective-permute-start.89 = (bf16[96,1536]{1,0:T(8,128)(2,1)S(1)}, bf16[96,1536]{1,0:T(8,128)(2,1)S(1)}, u32[]{:S(2)}, u32[]{:S(2)}) collective-permute-start(bf16[96,1536]{1,0:T(8,128)(2,1)S(1)} %get-tuple-element.59), channel_id=1, source_target_pairs={{0,4},{4,8},{8,12},{12,14},{14,10},{10,6},{6,2},{2,0},{1,5},{5,9},... | collective-permute-start | bytes 884744 | tf_op jit(solution)/shard_map/ppermute | solution.py:160
  744.4 30.0 %collective-permute-start.131 = (bf16[192,768]{1,0:T(8,128)(2,1)S(1)}, bf16[192,768]{1,0:T(8,128)(2,1)S(1)}, u32[]{:S(2)}, u32[]{:S(2)}) collective-permute-start(bf16[192,768]{1,0:T(8,128)(2,1)S(1)} %get-tuple-element.53), channel_id=1, source_target_pairs={{4,0},{8,4},{12,8},{14,12},{10,14},{6,10},{2,6},{0,2},{5,1},{9,5},... | collective-permute-start | bytes 884744 | tf_op jit(solution)/shard_map/ppermute | solution.py:160
  746.1 30.3 %collective-permute-start.117 = (bf16[192,768]{1,0:T(8,128)(2,1)S(1)}, bf16[192,768]{1,0:T(8,128)(2,1)S(1)}, u32[]{:S(2)}, u32[]{:S(2)}) collective-permute-start(bf16[192,768]{1,0:T(8,128)(2,1)S(1)} %get-tuple-element.51), channel_id=1, source_target_pairs={{0,4},{4,8},{8,12},{12,14},{14,10},{10,6},{6,2},{2,0},{1,5},{5,9},... | collective-permute-start | bytes 884744 | tf_op jit(solution)/shard_map/ppermute | solution.py:160
  801.2 31.0 %collective-permute-start.106 = (bf16[96,1536]{1,0:T(8,128)(2,1)S(1)}, bf16[96,1536]{1,0:T(8,128)(2,1)S(1)}, u32[]{:S(2)}, u32[]{:S(2)}) collective-permute-start(bf16[96,1536]{1,0:T(8,128)(2,1)S(1)} %collective-permute-done.105), channel_id=1, source_target_pairs={{4,0},{8,4},{12,8},{14,12},{10,14},{6,10},{2,6},{0,2},{5,1},{9,5},... | collective-permute-start | bytes 884744 | tf_op jit(solution)/shard_map/ppermute | solution.py:160
  803.0 31.3 %collective-permute-start.92 = (bf16[96,1536]{1,0:T(8,128)(2,1)S(1)}, bf16[96,1536]{1,0:T(8,128)(2,1)S(1)}, u32[]{:S(2)}, u32[]{:S(2)}) collective-permute-start(bf16[96,1536]{1,0:T(8,128)(2,1)S(1)} %collective-permute-done.91), channel_id=1, source_target_pairs={{0,4},{4,8},{8,12},{12,14},{14,10},{10,6},{6,2},{2,0},{1,5},{5,9},... | collective-permute-start | bytes 884744 | tf_op jit(solution)/shard_map/ppermute | solution.py:160
  (321 other events, 2450.8 us)

commit v2 on v1

v2 whole, which is shorter than its diff:
```python
import functools

import jax
import jax.numpy as jnp
from jax import lax
from jax.experimental import pallas as pl
from jax.experimental.pallas import tpu as pltpu
from jax.sharding import PartitionSpec as P

HEAD_DIM = 64
SYMBOLS = 24
SEQ = 160
PARTS = 2
EPS = 1e-05
SCALE = HEAD_DIM**-0.5
VMEM_LIMIT = 40 * 1024 * 1024

root_half = 0.7071067811865476
root_two_pi = 0.3989422804014327
BF = jnp.bfloat16
F32 = jnp.float32


def swap(value):
    return lax.ppermute(value, "tensor", [(0, 1), (1, 0)])


def dot(a, b):
    return jnp.dot(a, b, preferred_element_type=F32)


def dot_rows(a, b):
    return lax.dot_general(a, b, (((1,), (1,)), ((), ())), preferred_element_type=F32)


def dot_cols(a, b):
    return lax.dot_general(a, b, (((0,), (0,)), ((), ())), preferred_element_type=F32)


def in_order(core, own, other):
    first = core == 0
    return jnp.concatenate(
        [jnp.where(first, own, other), jnp.where(first, other, own)], axis=1
    )


def own_part(core, value):
    half = value.shape[1] // 2
    return jnp.where(core == 0, value[:, :half], value[:, half:])


def normalise(rows):
    centred = rows - jnp.mean(rows, axis=-1, keepdims=True)
    inv_root = lax.rsqrt(jnp.mean(centred * centred, axis=-1, keepdims=True) + EPS)
    return centred * inv_root, inv_root


def norm_back(grads, normal, inv_root, gain):
    scaled = grads * gain
    inner = (
        scaled
        - jnp.mean(scaled, axis=-1, keepdims=True)
        - normal * jnp.mean(scaled * normal, axis=-1, keepdims=True)
    )
    return inner * inv_root


def pair_masks(dtype):
    lane = lax.broadcasted_iota(jnp.int32, (1, 2 * HEAD_DIM), 1)
    return (lane < HEAD_DIM).astype(dtype), (lane >= HEAD_DIM).astype(dtype)


def attn_forward_kernel(choose, keep, start, marks, *refs):
    refs = list(refs)
    own, other = refs.pop(0), refs.pop(0)
    if choose:
        own_late, other_late = refs.pop(0), refs.pop(0)
    live, joint, output = refs.pop(0), refs.pop(0), refs.pop(0)
    chain = pl.program_id(0)
    tag = marks[2 + start + chain]
    core = marks[1]
    a, b = own[...], other[...]
    if choose:
        early = marks[0] == 0
        a = jnp.where(early, a, own_late[...])
        b = jnp.where(early, b, other_late[...])
    rows = in_order(core, a, b)
    q, k, v = [dot(rows, joint[tag, j]).astype(BF) for j in range(3)]
    key_live = live[0] > 0
    masks = pair_masks(BF)
    left = pair_masks(F32)[0] > 0
    pieces = []
    kept = []
    for at in range(0, q.shape[1], 2 * HEAD_DIM):
        span = slice(at, at + 2 * HEAD_DIM)
        q2, k2, v2 = q[:, span] * jnp.asarray(SCALE, BF), k[:, span], v[:, span]
        mixed = []
        for mask in masks:
            scores = jnp.where(key_live, dot_rows(q2 * mask, k2), -1000000000.0)
            shifted = jnp.exp(scores - jnp.max(scores, axis=-1, keepdims=True))
            probs = (shifted * (1.0 / jnp.sum(shifted, axis=-1, keepdims=True))).astype(BF)
            kept.append(probs)
            mixed.append(dot(probs, v2))
        pieces.append(jnp.where(left, mixed[0], mixed[1]).astype(BF))
    mixed = jnp.concatenate(pieces, axis=1)
    refs[0][...] = rows
    refs[1][...] = dot(mixed, output[tag]).astype(BF)
    if keep:
        refs[2][...] = jnp.concatenate([q, k, v], axis=1)
        for at, probs in enumerate(kept):
            refs[3][0, at] = probs
        refs[4][...] = mixed


def feed_forward_kernel(keep, start, marks, rows, part, other, gains, shifts, up, bias, down, *outs):
    tag = marks[2 + start + pl.program_id(0)]
    total = rows[...].astype(F32) + (part[...].astype(F32) + other[...].astype(F32))
    normal, inv_root = normalise(total)
    low = (normal * gains[0:1] + shifts[0:1]).astype(BF)
    pre = dot(low, up[tag]) + jnp.where(tag == 0, bias[0:1], bias[1:2]).astype(F32)
    cdf = 0.5 * (1.0 + lax.erf(pre * root_half))
    hidden = (pre * cdf).astype(BF)
    outs[0][...] = dot(hidden, down[tag]).astype(BF)
    outs[1][...] = normal
    if keep:
        outs[2][...] = inv_root
        outs[3][...] = low
        outs[4][...] = hidden
        outs[5][...] = (cdf + pre * jnp.exp(-0.5 * pre * pre) * root_two_pi).astype(BF)


def second_norm(normal, part, other, gains, shifts):
    first = normal[...] * gains[0:1] + shifts[0:1]
    return normalise(first + (part[...].astype(F32) + other[...].astype(F32)))


def last_norm_kernel(marks, normal, part, other, gains, shifts, out):
    second, _ = second_norm(normal, part, other, gains, shifts)
    out[...] = own_part(marks[1], (second * gains[1:2] + shifts[1:2]).astype(BF))


def add_sums(grads, normal, sums):
    @pl.when(pl.program_id(0) == 0)
    def _():
        sums[...] = jnp.zeros_like(sums)

    sums[0:1] += jnp.sum(grads * normal, axis=0, keepdims=True)
    sums[1:2] += jnp.sum(grads, axis=0, keepdims=True)


def feed_back_kernel(last, start, marks, *refs):
    refs = list(refs)
    normal, part, other, gains, shifts, own_cot, other_cot = refs[:7]
    refs = refs[7:]
    tag = marks[2 + start + pl.program_id(0)]
    core = marks[1]
    a, b = own_cot[...], other_cot[...]
    if last:
        late = marks[0] == 1
        a = jnp.where(late, a, refs.pop(0)[...])
        b = jnp.where(late, b, refs.pop(0)[...])
    slope, up, down = refs[:3]
    outs = refs[3:]
    grads = in_order(core, a, b).astype(F32)
    second, inv_root = second_norm(normal, part, other, gains, shifts)
    back = norm_back(grads, second, inv_root, gains[1:2])
    low = back.astype(BF)
    d_pre = (dot_rows(low, down[tag]) * slope[...].astype(F32)).astype(BF)
    outs[0][...] = back
    outs[1][...] = dot_rows(d_pre, up[tag]).astype(BF)
    if last:
        outs[2][...] = low
        outs[3][...] = d_pre
        outs[4][...] = own_part(core, (second * gains[1:2] + shifts[1:2]).astype(BF))
        add_sums(grads, second, outs[5])


def attn_back_kernel(
    last, start, marks, back, part, other, normal, inv_root, gains, joined, probs, joint, output, *outs
):
    tag = marks[2 + start + pl.program_id(0)]
    core = marks[1]
    grads = back[...] + (part[...].astype(F32) + other[...].astype(F32))
    back_one = norm_back(grads, normal[...], inv_root[...], gains[0:1])
    low = back_one.astype(BF)
    d_mixed = dot_rows(low, output[tag]).astype(BF)
    masks = pair_masks(BF)
    left = pair_masks(F32)[0] > 0
    width = d_mixed.shape[1]
    q, k, v = [joined[:, j * width : (j + 1) * width] for j in range(3)]
    pieces = [[], [], []]
    head = 0
    for at in range(0, width, 2 * HEAD_DIM):
        span = slice(at, at + 2 * HEAD_DIM)
        q2, k2, v2, m2 = q[:, span], k[:, span], v[:, span], d_mixed[:, span]
        found = []
        for mask in masks:
            held = probs[0, head]
            wide = held.astype(F32)
            head += 1
            d_probs = dot_rows(m2 * mask, v2)
            inner = jnp.sum(wide * d_probs, axis=-1, keepdims=True)
            d_scores = (wide * (d_probs - inner)).astype(BF)
            found.append(
                (dot(d_scores, k2) * SCALE, dot_cols(d_scores, q2) * SCALE, dot_cols(held, m2))
            )
        for j in range(3):
            pieces[j].append(jnp.where(left, found[0][j], found[1][j]).astype(BF))
    blocks = [jnp.concatenate(p, axis=1) for p in pieces]
    d_rows = sum(dot_rows(blocks[j], joint[tag, j]) for j in range(3)).astype(BF)
    outs[0][...] = own_part(core, back_one) + own_part(core, d_rows).astype(F32)
    outs[1][...] = own_part(1 - core, d_rows)
    if last:
        outs[2][...] = low
        outs[3][...] = jnp.concatenate(blocks, axis=1)
        add_sums(grads, normal[...], outs[4])


def run_chains(kernel, name, marks, chains, ins, outs, flops):
    specs = []
    for array, kind, first in ins:
        if kind == "rows":
            specs.append(
                pl.BlockSpec((SEQ, array.shape[1]), lambda i, *_, first=first: (first + i, 0))
            )
        elif kind == "chain":
            rest = array.shape[1:]
            specs.append(
                pl.BlockSpec(
                    (1,) + rest, lambda i, *_, first=first, n=len(rest): (first + i,) + (0,) * n
                )
            )
        else:
            specs.append(pl.BlockSpec(memory_space=pltpu.VMEM))
    shapes, out_specs = [], []
    for trailing, dtype, kind in outs:
        if kind == "rows":
            shapes.append(jax.ShapeDtypeStruct((chains * SEQ,) + trailing, dtype))
            out_specs.append(pl.BlockSpec((SEQ,) + trailing, lambda i, *_: (i, 0)))
        elif kind == "chain":
            shapes.append(jax.ShapeDtypeStruct((chains,) + trailing, dtype))
            out_specs.append(
                pl.BlockSpec((1,) + trailing, lambda i, *_, n=len(trailing): (i,) + (0,) * n)
            )
        else:
            shapes.append(jax.ShapeDtypeStruct(trailing, dtype))
            out_specs.append(pl.BlockSpec(trailing, lambda i, *_, n=len(trailing): (0,) * n))
    moved = sum(a.size * a.dtype.itemsize for a, _, _ in ins)
    moved += sum(s.size * s.dtype.itemsize for s in shapes)
    return pl.pallas_call(
        kernel,
        grid_spec=pltpu.PrefetchScalarGridSpec(
            num_scalar_prefetch=1, grid=(chains,), in_specs=specs, out_specs=out_specs
        ),
        out_shape=shapes,
        compiler_params=pltpu.CompilerParams(vmem_limit_bytes=VMEM_LIMIT),
        cost_estimate=pl.CostEstimate(
            flops=flops, bytes_accessed=moved, transcendentals=0
        ),
        name=name,
    )(marks, *[a for a, _, _ in ins])


def weight_pair(rows, grads, is_light):
    zero_rows = jnp.zeros_like(rows)
    heavy = dot_cols(jnp.where(is_light, zero_rows, rows), grads)
    light = dot_cols(jnp.where(is_light, rows, zero_rows), grads)
    return [heavy.astype(BF), light.astype(BF)]


def ring_order(count):
    return list(range(0, count, 2)) + list(range(1, count, 2))[::-1]


def ring_sum(heavy, light):
    count = lax.axis_size("dp")
    order = ring_order(count)
    rank = lax.axis_index("dp")
    place = jnp.zeros((), jnp.int32)
    for at, member in enumerate(order):
        place = jnp.where(rank == member, at, place)
    ahead = [(order[i], order[(i + 1) % count]) for i in range(count)]
    behind = [(b, a) for a, b in ahead]
    shape = heavy.shape
    rows = shape[0] // count

    def shard(whole, index):
        return lax.dynamic_slice_in_dim(whole, lax.rem(index, count) * rows, rows, 0)

    results = []
    for whole, pairs, sign in ((heavy, ahead, -1), (light, behind, 1)):
        moving = shard(whole, place + sign + count)
        for step in range(count - 1):
            moving = lax.ppermute(moving, "dp", pairs)
            index = place + sign * (step + 2) + 2 * count
            moving = (moving.astype(F32) + shard(whole, index).astype(F32)).astype(BF)
        out = jnp.zeros(shape, F32)
        index = place
        for step in range(count):
            out = lax.dynamic_update_slice_in_dim(
                out, moving.astype(F32), lax.rem(index, count) * rows, 0
            )
            if step < count - 1:
                moving = lax.ppermute(moving, "dp", pairs)
                index = place + sign * (step + 1) + count
        results.append(out)
    return jnp.stack(results)


def small_sum(value):
    count = lax.axis_size("dp")
    if count & (count - 1):
        return lax.psum(value, "dp")
    apart = 1
    while apart < count:
        value = value + lax.ppermute(value, "dp", [(i, i ^ apart) for i in range(count)])
        apart *= 2
    return value


def shards(
    chain_inputs,
    cotangent,
    chain_tags,
    pad_mask,
    predicted,
    target_ids,
    joint_proj,
    output_proj,
    up_proj,
    up_bias,
    down_proj,
    norm_gain,
    norm_shift,
):
    section = lax.axis_index("section")
    core = lax.axis_index("tensor")
    tokens, half = chain_inputs.shape
    width = 2 * half
    all_chains = tokens // SEQ
    chains = all_chains // PARTS
    light_all = (jnp.repeat(chain_tags, SEQ) > 0)[:, None]
    tags = (chain_tags > 0).astype(jnp.int32)
    marks = jnp.concatenate([jnp.stack([section, core]).astype(jnp.int32), tags])
    live = pad_mask.reshape(all_chains, 1, SEQ)
    joint = joint_proj[0].transpose(0, 2, 1, 3)
    output, up, bias, down = output_proj[0], up_proj[0], up_bias[0], down_proj[0]
    gains, shifts = norm_gain[0], norm_shift[0]
    units = up.shape[2]
    local = output.shape[1]
    heads = local // HEAD_DIM
    rows = chains * SEQ
    attn_flops = 2 * rows * (width * 4 * local + 2 * local * SEQ)
    feed_flops = 2 * rows * width * 2 * units

    cot_other = swap(cotangent)
    rows_other = swap(chain_inputs)

    def attn_forward(p, late, keep):
        start = p * chains
        ins = [(chain_inputs, "rows", start), (rows_other, "rows", start)]
        if late is not None:
            ins += [(late[0], "rows", 0), (late[1], "rows", 0)]
        ins += [(live, "chain", start), (joint, "whole", 0), (output, "whole", 0)]
        outs = [((width,), BF, "rows"), ((width,), BF, "rows")]
        if keep:
            outs += [
                ((3 * local,), BF, "rows"),
                ((heads, SEQ, SEQ), BF, "chain"),
                ((local,), BF, "rows"),
            ]
        kernel = functools.partial(attn_forward_kernel, late is not None, keep, start)
        return run_chains(kernel, "attn_forward", marks, chains, ins, outs, attn_flops)

    def feed_forward(p, x, part, keep):
        ins = [(x, "rows", 0), (part, "rows", 0), (swap(part), "rows", 0)]
        ins += [(a, "whole", 0) for a in (gains, shifts, up, bias, down)]
        outs = [((width,), BF, "rows"), ((width,), F32, "rows")]
        if keep:
            outs += [
                ((1,), F32, "rows"),
                ((width,), BF, "rows"),
                ((units,), BF, "rows"),
                ((units,), BF, "rows"),
            ]
        kernel = functools.partial(feed_forward_kernel, keep, p * chains)
        return run_chains(kernel, "feed_forward", marks, chains, ins, outs, feed_flops)

    def last_norm(p, normal, part):
        ins = [(normal, "rows", 0), (part, "rows", 0), (swap(part), "rows", 0)]
        ins += [(gains, "whole", 0), (shifts, "whole", 0)]
        return run_chains(
            last_norm_kernel, "last_norm", marks, chains, ins, [((half,), BF, "rows")], 0
        )[0]

    def feed_back(p, kept, late):
        ins = [(kept[n], "rows", 0) for n in ("normal", "down", "down_other")]
        ins += [(gains, "whole", 0), (shifts, "whole", 0)]
        ins += [(cotangent, "rows", p * chains), (cot_other, "rows", p * chains)]
        if late is not None:
            ins += [(late[0], "rows", 0), (late[1], "rows", 0)]
        ins += [(kept["slope"], "rows", 0), (up, "whole", 0), (down, "whole", 0)]
        outs = [((width,), F32, "rows"), ((width,), BF, "rows")]
        if late is not None:
            outs += [
                ((width,), BF, "rows"),
                ((units,), BF, "rows"),
                ((half,), BF, "rows"),
                ((2, width), F32, "whole"),
            ]
        kernel = functools.partial(feed_back_kernel, late is not None, p * chains)
        return run_chains(kernel, "feed_back", marks, chains, ins, outs, feed_flops)

    def attn_back(p, kept, back, part, last):
        ins = [(back, "rows", 0), (part, "rows", 0), (swap(part), "rows", 0)]
        ins += [(kept["normal"], "rows", 0), (kept["inv_root"], "rows", 0), (gains, "whole", 0)]
        ins += [(kept["joined"], "rows", 0), (kept["probs"], "chain", 0)]
        ins += [(joint, "whole", 0), (output, "whole", 0)]
        outs = [((half,), F32, "rows"), ((half,), BF, "rows")]
        if last:
            outs += [
                ((width,), BF, "rows"),
                ((3 * local,), BF, "rows"),
                ((2, width), F32, "whole"),
            ]
        kernel = functools.partial(attn_back_kernel, last, p * chains)
        return run_chains(kernel, "attn_back", marks, chains, ins, outs, attn_flops)

    parts = range(PARTS)
    attn = [attn_forward(p, None, False) for p in parts]
    feed = [feed_forward(p, attn[p][0], attn[p][1], False) for p in parts]
    late = []
    for p in parts:
        moved = lax.ppermute(last_norm(p, feed[p][1], feed[p][0]), "section", [(0, 1)])
        late.append((moved, swap(moved)))
    attn = [attn_forward(p, late[p], True) for p in parts]
    kept = []
    for p in parts:
        x, part, joined, probs, mixed = attn[p]
        down_part, normal, inv_root, low, hidden, slope = feed_forward(p, x, part, True)
        kept.append(
            dict(
                rows=x,
                joined=joined,
                probs=probs,
                mixed=mixed,
                down=down_part,
                down_other=swap(down_part),
                normal=normal,
                inv_root=inv_root,
                low=low,
                hidden=hidden,
                slope=slope,
            )
        )
    feed = [feed_back(p, kept[p], None) for p in parts]
    late = []
    for p in parts:
        mine, theirs = attn_back(p, kept[p], feed[p][0], feed[p][1], False)
        total = (mine + swap(theirs).astype(F32)).astype(BF)
        moved = lax.ppermute(total, "section", [(1, 0)])
        late.append((moved, swap(moved)))
    feed = [feed_back(p, kept[p], late[p]) for p in parts]
    attn = [attn_back(p, kept[p], feed[p][0], feed[p][1], True) for p in parts]
    input_grads = jnp.concatenate(
        [attn[p][0] + swap(attn[p][1]).astype(F32) for p in parts], axis=0
    )

    def whole(pieces):
        return jnp.concatenate(pieces, axis=0)

    d_pre = whole([f[3] for f in feed])
    down_sum = ring_sum(
        *weight_pair(whole([k["hidden"] for k in kept]), whole([f[2] for f in feed]), light_all)
    )
    up_sum = ring_sum(*weight_pair(whole([k["low"] for k in kept]), d_pre, light_all))
    output_sum = ring_sum(
        *weight_pair(whole([k["mixed"] for k in kept]), whole([a[2] for a in attn]), light_all)
    )
    pair = weight_pair(whole([k["rows"] for k in kept]), whole([a[3] for a in attn]), light_all)
    pair = [g.reshape(width, 3, local).transpose(1, 0, 2).reshape(3 * width, local) for g in pair]
    joint_sum = ring_sum(*pair).reshape(2, 3, width, local).transpose(0, 2, 1, 3)

    pre_wide = d_pre.astype(F32)
    zero = jnp.zeros_like(pre_wide)
    bias_grad = jnp.stack(
        [
            jnp.sum(jnp.where(light_all, zero, pre_wide), 0),
            jnp.sum(jnp.where(light_all, pre_wide, zero), 0),
        ]
    )
    sums_two = sum(f[5] for f in feed)
    sums_one = sum(a[4] for a in attn)
    sums = jnp.stack([sums_one, sums_two], axis=1)
    symbols = jnp.arange(SYMBOLS, dtype=jnp.int32)
    target_hits = (target_ids[:, None] == symbols[None, :]) & (pad_mask[:, None] > 0)
    correct_hits = target_hits & (predicted == target_ids)[:, None]
    counts = jnp.stack([jnp.sum(target_hits, 0), jnp.sum(correct_hits, 0)]).astype(F32)
    small = [bias_grad, sums, counts]
    packed = small_sum(jnp.concatenate([s.reshape(-1) for s in small]))
    results = []
    at = 0
    for s in small:
        results.append(packed[at : at + s.size].reshape(s.shape))
        at += s.size
    bias_grad, sums, counts = results
    return (
        whole([f[4] for f in feed])[None],
        input_grads[None],
        joint_sum[None],
        output_sum[None],
        up_sum[None],
        bias_grad[None],
        down_sum[None],
        sums[0][None],
        sums[1][None],
        counts.astype(jnp.int32),
    )


def solution(mesh):
    return jax.shard_map(
        shards,
        mesh=mesh,
        in_specs=(
            P("dp", "tensor"),
            P("dp", "tensor"),
            P("dp"),
            P("dp"),
            P("dp"),
            P("dp"),
            P("section", None, None, None, "tensor"),
            P("section", None, "tensor", None),
            P("section", None, None, "tensor"),
            P("section", None, "tensor"),
            P("section", None, "tensor", None),
            P("section", None, None),
            P("section", None, None),
        ),
        out_specs=(
            P("section", "dp", "tensor"),
            P("section", "dp", "tensor"),
            P("section", None, None, None, "tensor"),
            P("section", None, "tensor", None),
            P("section", None, None, "tensor"),
            P("section", None, "tensor"),
            P("section", None, "tensor", None),
            P("section", None, None),
            P("section", None, None),
            P(),
        ),
        check_vma=False,
    )
```

time: 887 us -> 658 us (0.74)
  matrix products: 207 us -> 27 us
  Pallas kernels: 0 us -> 141 us
  local copies, waits for them, and re-layouts: 174 us -> 69.1 us
  other arithmetic: 107 us -> 50.7 us
  blocking collectives: 36.8 us -> 0 us
  starting transfers between devices: 132 us -> 141 us
    dot_general x96 -> x8, matrix products: 207 us -> 27 us  [dot_cols(): lax.dot_general(a, b, (((0,), (0,)), ((), ())), preferred_element_type=F32)]
    pallas_call x0 -> x18, Pallas kernels: none -> 141 us  [run_chains(): pl.pallas_call(kernel, grid_spec=pltpu.PrefetchScalarGridSpec(num_scalar_...]
    reshape x19 -> x3, local copies, waits for them, and re-layouts: 43 us -> 0.86 us  [the longest x1 0.83 us: shards(): live = pad_mask.reshape(all_chains, 1, SEQ)]
    psum x1 -> x0, blocking collectives: 36.8 us -> none  [shards(): packed = lax.psum(packed, 'dp')]
    convert_element_type x12 -> x2, local copies, waits for them, and re-layouts: 38.5 us -> 5.24 us  [weight_pair(): return [heavy.astype(BF), light.astype(BF)]]
    reduce_sum x22 -> x0, other arithmetic: 25.6 us -> none  [the longest x4 12 us: norm_back(): jnp.mean(scaled, axis=-1, keepdims=True)]
    slice x16 -> x4, local copies, waits for them, and re-layouts: 18.5 us -> 1.21 us  [the longest x2 0.61 us: shards(): sums[1][None]]
    convert_element_type x14 -> x2, other arithmetic: 15 us -> 0.2 us  [shards(): total = (mine + swap(theirs).astype(F32)).astype(BF)]
  transfers between devices with their start and end apart: 138 -> 141, of which waited for: 69 -> 63; matrix products, arithmetic and copies ran while one was open for 35% -> 13% of each run, Pallas kernels for 0% -> 19%
where the time goes in v2:
time: 658 us; the launch traced here: 651 us
  waiting for transfers between devices  219 us (33%)
  starting transfers between devices  141 us (21%)
  Pallas kernels  141 us (21%)
  local copies, waits for them, and re-layouts  69.1 us (11%)
  other arithmetic  50.7 us (8%)
  matrix products  27 us (4%)
    ppermute x112, waiting for transfers between devices, ring_sum(): moving = lax.ppermute(moving, 'dp', pairs)  185 us
    pallas_call x18, Pallas kernels, run_chains(): pl.pallas_call(kernel, grid_spec=pltpu.PrefetchScalarGridSpec(num_scalar_...  141 us
    ppermute x112, starting transfers between devices, ring_sum(): moving = lax.ppermute(moving, 'dp', pairs)  120 us
    unnamed x194, local copies, waits for them, and re-layouts  40.5 us
    dot_general x8, matrix products, dot_cols(): lax.dot_general(a, b, (((0,), (0,)), ((), ())), preferred_element_type=F32)  27 us
    convert_element_type x48, other arithmetic, ring_sum(): moving = (moving.astype(F32) + shard(whole, index).astype(F32)).astype(BF)  24 us
    ppermute x2, waiting for transfers between devices, shards(): moved = lax.ppermute(total, 'section', [(1, 0)])  17.7 us
    ppermute x2, waiting for transfers between devices, shards(): lax.ppermute(last_norm(p, feed[p][1], feed[p][0]), 'section', [(0, 1)])  13.2 us
  transfers between devices with their start and end apart: 141, of which 63 were waited for; matrix products, arithmetic and copies ran while one was open for 13% of the time, Pallas kernels for 19%

profile of v2, /device:TPU:0, one launch (start us, length us, event | category | flops | bytes accessed | tf_op | source)
XLA Modules:
  0.0 650.7 jit_solution(11070233155373767872)
XLA Ops:
  41.5 6.1 collective-permute-done.3.refs_2_
  47.6 7.1 %collective-permute-done.14.refs_2_ = bf16[480,384]{1,0:T(8,128)(2,1)S(1)} collective-permute-done((bf16[480,384]{1,0:T(8,128)(2,1)S(1)}, bf16[480,384]{1,0:T(8,128)(2,1)S(1)}, u32[]{:S(2)}, u32[]{:S(2)}) %collective-permute-start.14) | collective-permute-done | bytes 368672 | tf_op jit(solution)/shard_map/ppermute | solution.py:434
  54.7 5.1 attn_forward.5
  70.0 7.6 %feed_forward.5 = (bf16[480,768]{1,0:T(8,128)(2,1)}, f32[480,768]{1,0:T(8,128)S(1)}, f32[480,1]{1,0:T(8,128)S(1)}, bf16[480,768]{1,0:T(8,128)(2,1)S(1)}, bf16[48...) custom-call(s32[8]{0:T(128)S(1)} %pad_add_fusion.marks, bf16[480,768]{1,0:T(8,128)(2,1)S(1)} %get-tuple-element.74.rows, ...), custom_call_target="tpu_custom_call" | custom-call | flops 2264924160 | bytes 17567616 | tf_op jit(solution)/shard_map/feed_forward/pallas_call | solution.py:250
  80.8 7.6 %feed_forward.7 = (bf16[480,768]{1,0:T(8,128)(2,1)}, f32[480,768]{1,0:T(8,128)S(1)}, f32[480,1]{1,0:T(8,128)S(1)}, bf16[480,768]{1,0:T(8,128)(2,1)S(1)}, bf16[48...) custom-call(s32[8]{0:T(128)S(1)} %pad_add_fusion.marks, bf16[480,768]{1,0:T(8,128)(2,1)S(1)} %get-tuple-element.91.rows, ...), custom_call_target="tpu_custom_call" | custom-call | flops 2264924160 | bytes 17567616 | tf_op jit(solution)/shard_map/feed_forward/pallas_call | solution.py:250
  97.4 10.1 %feed_back.4 = (f32[480,768]{1,0:T(8,128)S(1)}, bf16[480,768]{1,0:T(8,128)(2,1)}) custom-call(s32[8]{0:T(128)S(1)} %pad_add_fusion.marks, f32[480,768]{1,0:T(8,128)S(1)} %get-tuple-element.76.refs_0_.normal, bf16[480,768]{1,0:T(8,128)(2,1)} %get-tuple-element.77.refs_1_, bf16[480,768]{1,0:T(8,128)(2,1)} %collective-permute-done.6.refs_2_, ...), custom_call_target="tpu_custom_call" | custom-call | flops 2264924160 | bytes 17559552 | tf_op jit(solution)/shard_map/feed_back/pallas_call | solution.py:250
  107.7 10.1 %feed_back.6 = (f32[480,768]{1,0:T(8,128)S(1)}, bf16[480,768]{1,0:T(8,128)(2,1)}) custom-call(s32[8]{0:T(128)S(1)} %pad_add_fusion.marks, f32[480,768]{1,0:T(8,128)S(1)} %get-tuple-element.93.refs_0_.normal, bf16[480,768]{1,0:T(8,128)(2,1)} %get-tuple-element.94.refs_1_, bf16[480,768]{1,0:T(8,128)(2,1)} %collective-permute-done.17.refs_2_, ...), custom_call_target="tpu_custom_call" | custom-call | flops 2264924160 | bytes 17559552 | tf_op jit(solution)/shard_map/feed_back/pallas_call | solution.py:250
  134.3 11.9 %attn_back.4 = (f32[480,384]{1,0:T(8,128)S(1)}, bf16[480,384]{1,0:T(8,128)(2,1)S(1)}) custom-call(s32[8]{0:T(128)S(1)} %copy-done.66, f32[480,768]{1,0:T(8,128)S(1)} %copy-done.45, bf16[480,768]{1,0:T(8,128)(2,1)} %get-tuple-element.80.part, bf16[480,768]{1,0:T(8,128)(2,1)} %collective-permute-done.8.other, f32[480,768]{1,0:T(8,128)S(1)} %copy-done.14, ...), custom_call_target="tpu_custom_call" | custom-call | flops 1250426880 | bytes 12283776 | tf_op jit(solution)/shard_map/attn_back/pallas_call | solution.py:250
  146.7 11.6 %attn_back.5 = (f32[480,384]{1,0:T(8,128)S(1)}, bf16[480,384]{1,0:T(8,128)(2,1)S(1)}) custom-call(s32[8]{0:T(128)S(1)} %copy-done.66, f32[480,768]{1,0:T(8,128)S(1)} %copy-done.43, bf16[480,768]{1,0:T(8,128)(2,1)} %get-tuple-element.97.part, bf16[480,768]{1,0:T(8,128)(2,1)} %collective-permute-done.18.other, f32[480,768]{1,0:T(8,128)S(1)} %copy-done.11, ...), custom_call_target="tpu_custom_call" | custom-call | flops 1250426880 | bytes 12283776 | tf_op jit(solution)/shard_map/attn_back/pallas_call | solution.py:250
  161.8 10.3 %collective-permute-done.10.refs_7_ = bf16[480,384]{1,0:T(8,128)(2,1)S(1)} collective-permute-done((bf16[480,384]{1,0:T(8,128)(2,1)S(1)}, bf16[480,384]{1,0:T(8,128)(2,1)S(1)}, u32[]{:S(2)}, u32[]{:S(2)}) %collective-permute-start.10) | collective-permute-done | bytes 368672 | tf_op jit(solution)/shard_map/ppermute | solution.py:461
  172.3 7.4 %collective-permute-done.20.refs_7_ = bf16[480,384]{1,0:T(8,128)(2,1)S(1)} collective-permute-done((bf16[480,384]{1,0:T(8,128)(2,1)S(1)}, bf16[480,384]{1,0:T(8,128)(2,1)S(1)}, u32[]{:S(2)}, u32[]{:S(2)}) %collective-permute-start.20) | collective-permute-done | bytes 368672 | tf_op jit(solution)/shard_map/ppermute | solution.py:461
  179.7 12.3 %feed_back.5 = (f32[480,768]{1,0:T(8,128)S(1)}, bf16[480,768]{1,0:T(8,128)(2,1)}, bf16[480,768]{1,0:T(8,128)(2,1)S(1)}, bf16[480,1536]{1,0:T(8,128)(2,1)S(1)}, b...) custom-call(s32[8]{0:T(128)S(1)} %copy-done.66, f32[480,768]{1,0:T(8,128)S(1)} %copy-done.15, ...), custom_call_target="tpu_custom_call" | custom-call | flops 2264924160 | bytes 20883456 | tf_op jit(solution)/shard_map/feed_back/pallas_call | solution.py:250
  194.0 11.9 %feed_back.7 = (f32[480,768]{1,0:T(8,128)S(1)}, bf16[480,768]{1,0:T(8,128)(2,1)}, bf16[480,768]{1,0:T(8,128)(2,1)S(1)}, bf16[480,1536]{1,0:T(8,128)(2,1)S(1)}, b...) custom-call(s32[8]{0:T(128)S(1)} %copy-done.66, f32[480,768]{1,0:T(8,128)S(1)} %copy-done.11, ...), custom_call_target="tpu_custom_call" | custom-call | flops 2264924160 | bytes 20883456 | tf_op jit(solution)/shard_map/feed_back/pallas_call | solution.py:250
  257.7 13.4 %attn_back.6 = (f32[480,384]{1,0:T(8,128)S(1)}, bf16[480,384]{1,0:T(8,128)(2,1)S(1)}, bf16[480,768]{1,0:T(8,128)(2,1)S(1)}, bf16[480,1152]{1,0:T(8,128)(2,1)S(1)}, f32[2,768]{1,0:T(2,128)S(1)}) custom-call(s32[8]{0:T(128)S(1)} %copy-done.67, f32[480,768]{1,0:T(8,128)S(1)} %copy-done.47, bf16[480,768]{1,0:T(8,128)(2,1)} %get-tuple-element.105.part, ...), custom_call_target="tpu_custom_call" | custom-call | flops 1250426880 | bytes 14133120 | tf_op jit(solution)/shard_map/attn_back/pallas_call | solution.py:250
  272.7 13.2 %attn_back.7 = (f32[480,384]{1,0:T(8,128)S(1)}, bf16[480,384]{1,0:T(8,128)(2,1)S(1)}, bf16[480,768]{1,0:T(8,128)(2,1)S(1)}, bf16[480,1152]{1,0:T(8,128)(2,1)S(1)}, f32[2,768]{1,0:T(2,128)S(1)}) custom-call(s32[8]{0:T(128)S(1)} %copy-done.67, f32[480,768]{1,0:T(8,128)S(1)} %get-tuple-element.108.back, bf16[480,768]{1,0:T(8,128)(2,1)} %get-tuple-element.109.part, ...), custom_call_target="tpu_custom_call" | custom-call | flops 1250426880 | bytes 14133120 | tf_op jit(solution)/shard_map/attn_back/pallas_call | solution.py:250
  323.1 5.5 collective-permute-done.68
  423.2 6.7 %collective-permute-done.42 = bf16[288,384]{1,0:T(8,128)(2,1)S(1)} collective-permute-done((bf16[288,384]{1,0:T(8,128)(2,1)S(1)}, bf16[288,384]{1,0:T(8,128)(2,1)S(1)}, u32[]{:S(2)}, u32[]{:S(2)}) %collective-permute-start.42) | collective-permute-done | bytes 221216 | tf_op jit(solution)/shard_map/ppermute | solution.py:294
  452.0 7.3 %collective-permute-done.78 = bf16[48,768]{1,0:T(8,128)(2,1)S(1)} collective-permute-done((bf16[48,768]{1,0:T(8,128)(2,1)S(1)}, bf16[48,768]{1,0:T(8,128)(2,1)S(1)}, u32[]{:S(2)}, u32[]{:S(2)}) %collective-permute-start.78) | collective-permute-done | bytes 73760 | tf_op jit(solution)/shard_map/ppermute | solution.py:304
  466.6 7.5 %collective-permute-done.79 = bf16[48,768]{1,0:T(8,128)(2,1)S(1)} collective-permute-done((bf16[48,768]{1,0:T(8,128)(2,1)S(1)}, bf16[48,768]{1,0:T(8,128)(2,1)S(1)}, u32[]{:S(2)}, u32[]{:S(2)}) %collective-permute-start.79) | collective-permute-done | bytes 73760 | tf_op jit(solution)/shard_map/ppermute | solution.py:304
  474.1 5.6 collective-permute-done.65
  519.1 13.1 %collective-permute-done.32 = bf16[288,384]{1,0:T(8,128)(2,1)S(1)} collective-permute-done((bf16[288,384]{1,0:T(8,128)(2,1)S(1)}, bf16[288,384]{1,0:T(8,128)(2,1)S(1)}, u32[]{:S(2)}, u32[]{:S(2)}) %collective-permute-start.32) | collective-permute-done | bytes 221216 | tf_op jit(solution)/shard_map/ppermute | solution.py:294
  534.6 5.9 collective-permute-done.46
  565.2 5.2 collective-permute-done.136
  584.0 15.2 %collective-permute-done.36 = bf16[288,384]{1,0:T(8,128)(2,1)S(1)} collective-permute-done((bf16[288,384]{1,0:T(8,128)(2,1)S(1)}, bf16[288,384]{1,0:T(8,128)(2,1)S(1)}, u32[]{:S(2)}, u32[]{:S(2)}) %collective-permute-start.36) | collective-permute-done | bytes 221216 | tf_op jit(solution)/shard_map/ppermute | solution.py:304
  (660 shorter events, 429.8 us)
Async XLA Ops:
  118.9 27.7 %collective-permute-start.18 = (bf16[480,768]{1,0:T(8,128)(2,1)}, bf16[480,768]{1,0:T(8,128)(2,1)}, u32[]{:S(2)}, u32[]{:S(2)}) collective-permute-start(bf16[480,768]{1,0:T(8,128)(2,1)} %get-tuple-element.97.part), channel_id=1, source_target_pairs={{0,1},{1,0},{2,3},{3,2},{4,5},{5,4},{6,7},{7,6},{8,9},{9,8},{10,11... | collective-permute-start | bytes 2211848 | tf_op jit(solution)/shard_map/ppermute | solution.py:25
  225.6 32.0 %collective-permute-start.22 = (bf16[480,768]{1,0:T(8,128)(2,1)}, bf16[480,768]{1,0:T(8,128)(2,1)}, u32[]{:S(2)}, u32[]{:S(2)}) collective-permute-start(bf16[480,768]{1,0:T(8,128)(2,1)} %get-tuple-element.105.part), channel_id=1, source_target_pairs={{0,1},{1,0},{2,3},{3,2},{4,5},{5,4},{6,7},{7,6},{8,9},{9,8},{10,11... | collective-permute-start | bytes 2211848 | tf_op jit(solution)/shard_map/ppermute | solution.py:25
  225.6 45.5 %collective-permute-start.24 = (bf16[480,768]{1,0:T(8,128)(2,1)}, bf16[480,768]{1,0:T(8,128)(2,1)}, u32[]{:S(2)}, u32[]{:S(2)}) collective-permute-start(bf16[480,768]{1,0:T(8,128)(2,1)} %get-tuple-element.109.part), channel_id=1, source_target_pairs={{0,1},{1,0},{2,3},{3,2},{4,5},{5,4},{6,7},{7,6},{8,9},{9,8},{10,11... | collective-permute-start | bytes 2211848 | tf_op jit(solution)/shard_map/ppermute | solution.py:25
  249.0 91.5 %collective-permute-start.115 = (bf16[192,768]{1,0:T(8,128)(2,1)}, bf16[192,768]{1,0:T(8,128)(2,1)}, u32[]{:S(2)}, u32[]{:S(2)}) collective-permute-start(bf16[192,768]{1,0:T(8,128)(2,1)} %add_convert_fusion.14), channel_id=1, source_target_pairs={{0,4},{4,8},{8,12},{12,14},{14,10},{10,6},{6,2},{2,0},{1,5},{5,9},... | collective-permute-start | bytes 884744 | tf_op jit(solution)/shard_map/ppermute | solution.py:294
  251.9 90.1 %collective-permute-start.129 = (bf16[192,768]{1,0:T(8,128)(2,1)}, bf16[192,768]{1,0:T(8,128)(2,1)}, u32[]{:S(2)}, u32[]{:S(2)}) collective-permute-start(bf16[192,768]{1,0:T(8,128)(2,1)} %add_convert_fusion.7), channel_id=1, source_target_pairs={{4,0},{8,4},{12,8},{14,12},{10,14},{6,10},{2,6},{0,2},{5,1},{9,5},... | collective-permute-start | bytes 884744 | tf_op jit(solution)/shard_map/ppermute | solution.py:294
  255.3 82.2 %collective-permute-start.84 = (bf16[96,1536]{1,0:T(8,128)(2,1)}, bf16[96,1536]{1,0:T(8,128)(2,1)}, u32[]{:S(2)}, u32[]{:S(2)}) collective-permute-start(bf16[96,1536]{1,0:T(8,128)(2,1)} %add_convert_fusion.28), channel_id=1, source_target_pairs={{0,4},{4,8},{8,12},{12,14},{14,10},{10,6},{6,2},{2,0},{1,5},{5,9},... | collective-permute-start | bytes 884744 | tf_op jit(solution)/shard_map/ppermute | solution.py:294
  339.2 35.7 %collective-permute-start.23 = (bf16[480,384]{1,0:T(8,128)(2,1)S(1)}, bf16[480,384]{1,0:T(8,128)(2,1)S(1)}, u32[]{:S(2)}, u32[]{:S(2)}) collective-permute-start(bf16[480,384]{1,0:T(8,128)(2,1)S(1)} %get-tuple-element.107), channel_id=1, source_target_pairs={{0,1},{1,0},{2,3},{3,2},{4,5},{5,4},{6,7},{7,6},{8,9},{9,8},{10,11... | collective-permute-start | bytes 1105928 | tf_op jit(solution)/shard_map/ppermute | solution.py:25
  340.5 34.9 %collective-permute-start.25 = (bf16[480,384]{1,0:T(8,128)(2,1)S(1)}, bf16[480,384]{1,0:T(8,128)(2,1)S(1)}, u32[]{:S(2)}, u32[]{:S(2)}) collective-permute-start(bf16[480,384]{1,0:T(8,128)(2,1)S(1)} %get-tuple-element.111), channel_id=1, source_target_pairs={{0,1},{1,0},{2,3},{3,2},{4,5},{5,4},{6,7},{7,6},{8,9},{9,8},{10,11... | collective-permute-start | bytes 1105928 | tf_op jit(solution)/shard_map/ppermute | solution.py:25
  351.1 40.3 %collective-permute-start.116 = (bf16[192,768]{1,0:T(8,128)(2,1)S(1)}, bf16[192,768]{1,0:T(8,128)(2,1)S(1)}, u32[]{:S(2)}, u32[]{:S(2)}) collective-permute-start(bf16[192,768]{1,0:T(8,128)(2,1)S(1)} %add_convert_fusion.13), channel_id=1, source_target_pairs={{0,4},{4,8},{8,12},{12,14},{14,10},{10,6},{6,2},{2,0},{1,5},{5,9},... | collective-permute-start | bytes 884744 | tf_op jit(solution)/shard_map/ppermute | solution.py:294
  353.5 38.0 %collective-permute-start.130 = (bf16[192,768]{1,0:T(8,128)(2,1)S(1)}, bf16[192,768]{1,0:T(8,128)(2,1)S(1)}, u32[]{:S(2)}, u32[]{:S(2)}) collective-permute-start(bf16[192,768]{1,0:T(8,128)(2,1)S(1)} %add_convert_fusion.6), channel_id=1, source_target_pairs={{4,0},{8,4},{12,8},{14,12},{10,14},{6,10},{2,6},{0,2},{5,1},{9,5},... | collective-permute-start | bytes 884744 | tf_op jit(solution)/shard_map/ppermute | solution.py:294
  391.5 52.5 %collective-permute-start.117 = (bf16[192,768]{1,0:T(8,128)(2,1)S(1)}, bf16[192,768]{1,0:T(8,128)(2,1)S(1)}, u32[]{:S(2)}, u32[]{:S(2)}) collective-permute-start(bf16[192,768]{1,0:T(8,128)(2,1)S(1)} %add_convert_fusion.12), channel_id=1, source_target_pairs={{0,4},{4,8},{8,12},{12,14},{14,10},{10,6},{6,2},{2,0},{1,5},{5,9},... | collective-permute-start | bytes 884744 | tf_op jit(solution)/shard_map/ppermute | solution.py:294
  393.7 50.9 %collective-permute-start.131 = (bf16[192,768]{1,0:T(8,128)(2,1)S(1)}, bf16[192,768]{1,0:T(8,128)(2,1)S(1)}, u32[]{:S(2)}, u32[]{:S(2)}) collective-permute-start(bf16[192,768]{1,0:T(8,128)(2,1)S(1)} %add_convert_fusion.5), channel_id=1, source_target_pairs={{4,0},{8,4},{12,8},{14,12},{10,14},{6,10},{2,6},{0,2},{5,1},{9,5},... | collective-permute-start | bytes 884744 | tf_op jit(solution)/shard_map/ppermute | solution.py:294
  395.8 45.9 %collective-permute-start.86 = (bf16[96,1536]{1,0:T(8,128)(2,1)S(1)}, bf16[96,1536]{1,0:T(8,128)(2,1)S(1)}, u32[]{:S(2)}, u32[]{:S(2)}) collective-permute-start(bf16[96,1536]{1,0:T(8,128)(2,1)S(1)} %add_convert_fusion.26), channel_id=1, source_target_pairs={{0,4},{4,8},{8,12},{12,14},{14,10},{10,6},{6,2},{2,0},{1,5},{5,9},... | collective-permute-start | bytes 884744 | tf_op jit(solution)/shard_map/ppermute | solution.py:294
  397.6 44.6 %collective-permute-start.100 = (bf16[96,1536]{1,0:T(8,128)(2,1)S(1)}, bf16[96,1536]{1,0:T(8,128)(2,1)S(1)}, u32[]{:S(2)}, u32[]{:S(2)}) collective-permute-start(bf16[96,1536]{1,0:T(8,128)(2,1)S(1)} %add_convert_fusion.19), channel_id=1, source_target_pairs={{4,0},{8,4},{12,8},{14,12},{10,14},{6,10},{2,6},{0,2},{5,1},{9,5},... | collective-permute-start | bytes 884744 | tf_op jit(solution)/shard_map/ppermute | solution.py:294
  444.6 47.3 %collective-permute-start.118 = (bf16[192,768]{1,0:T(8,128)(2,1)S(1)}, bf16[192,768]{1,0:T(8,128)(2,1)S(1)}, u32[]{:S(2)}, u32[]{:S(2)}) collective-permute-start(bf16[192,768]{1,0:T(8,128)(2,1)S(1)} %add_convert_fusion.11), channel_id=1, source_target_pairs={{0,4},{4,8},{8,12},{12,14},{14,10},{10,6},{6,2},{2,0},{1,5},{5,9},... | collective-permute-start | bytes 884744 | tf_op jit(solution)/shard_map/ppermute | solution.py:294
  451.0 42.8 %collective-permute-start.132 = (bf16[192,768]{1,0:T(8,128)(2,1)S(1)}, bf16[192,768]{1,0:T(8,128)(2,1)S(1)}, u32[]{:S(2)}, u32[]{:S(2)}) collective-permute-start(bf16[192,768]{1,0:T(8,128)(2,1)S(1)} %add_convert_fusion.4), channel_id=1, source_target_pairs={{4,0},{8,4},{12,8},{14,12},{10,14},{6,10},{2,6},{0,2},{5,1},{9,5},... | collective-permute-start | bytes 884744 | tf_op jit(solution)/shard_map/ppermute | solution.py:294
  507.0 35.0 %collective-permute-start.120 = (bf16[192,768]{1,0:T(8,128)(2,1)S(1)}, bf16[192,768]{1,0:T(8,128)(2,1)S(1)}, u32[]{:S(2)}, u32[]{:S(2)}) collective-permute-start(bf16[192,768]{1,0:T(8,128)(2,1)S(1)} %get-tuple-element.135), channel_id=1, source_target_pairs={{0,4},{4,8},{8,12},{12,14},{14,10},{10,6},{6,2},{2,0},{1,5},{5,9},... | collective-permute-start | bytes 884744 | tf_op jit(solution)/shard_map/ppermute | solution.py:304
  510.1 34.2 %collective-permute-start.134 = (bf16[192,768]{1,0:T(8,128)(2,1)S(1)}, bf16[192,768]{1,0:T(8,128)(2,1)S(1)}, u32[]{:S(2)}, u32[]{:S(2)}) collective-permute-start(bf16[192,768]{1,0:T(8,128)(2,1)S(1)} %get-tuple-element.137), channel_id=1, source_target_pairs={{4,0},{8,4},{12,8},{14,12},{10,14},{6,10},{2,6},{0,2},{5,1},{9,5},... | collective-permute-start | bytes 884744 | tf_op jit(solution)/shard_map/ppermute | solution.py:304
  513.3 30.7 %collective-permute-start.89 = (bf16[96,1536]{1,0:T(8,128)(2,1)S(1)}, bf16[96,1536]{1,0:T(8,128)(2,1)S(1)}, u32[]{:S(2)}, u32[]{:S(2)}) collective-permute-start(bf16[96,1536]{1,0:T(8,128)(2,1)S(1)} %get-tuple-element.139), channel_id=1, source_target_pairs={{0,4},{4,8},{8,12},{12,14},{14,10},{10,6},{6,2},{2,0},{1,5},{5,9},... | collective-permute-start | bytes 884744 | tf_op jit(solution)/shard_map/ppermute | solution.py:304
  514.8 29.8 %collective-permute-start.103 = (bf16[96,1536]{1,0:T(8,128)(2,1)S(1)}, bf16[96,1536]{1,0:T(8,128)(2,1)S(1)}, u32[]{:S(2)}, u32[]{:S(2)}) collective-permute-start(bf16[96,1536]{1,0:T(8,128)(2,1)S(1)} %get-tuple-element.141), channel_id=1, source_target_pairs={{4,0},{8,4},{12,8},{14,12},{10,14},{6,10},{2,6},{0,2},{5,1},{9,5},... | collective-permute-start | bytes 884744 | tf_op jit(solution)/shard_map/ppermute | solution.py:304
  572.0 33.2 %collective-permute-start.137 = (bf16[192,768]{1,0:T(8,128)(2,1)S(1)}, bf16[192,768]{1,0:T(8,128)(2,1)S(1)}, u32[]{:S(2)}, u32[]{:S(2)}) collective-permute-start(bf16[192,768]{1,0:T(8,128)(2,1)S(1)} %collective-permute-done.136), channel_id=1, source_target_pairs={{4,0},{8,4},{12,8},{14,12},{10,14},{6,10},{2,6},{0,2},{5,1},{9,5},... | collective-permute-start | bytes 884744 | tf_op jit(solution)/shard_map/ppermute | solution.py:304
  577.1 30.2 %collective-permute-start.92 = (bf16[96,1536]{1,0:T(8,128)(2,1)S(1)}, bf16[96,1536]{1,0:T(8,128)(2,1)S(1)}, u32[]{:S(2)}, u32[]{:S(2)}) collective-permute-start(bf16[96,1536]{1,0:T(8,128)(2,1)S(1)} %collective-permute-done.91), channel_id=1, source_target_pairs={{0,4},{4,8},{8,12},{12,14},{14,10},{10,6},{6,2},{2,0},{1,5},{5,9},... | collective-permute-start | bytes 884744 | tf_op jit(solution)/shard_map/ppermute | solution.py:304
  577.1 32.3 %collective-permute-start.123 = (bf16[192,768]{1,0:T(8,128)(2,1)S(1)}, bf16[192,768]{1,0:T(8,128)(2,1)S(1)}, u32[]{:S(2)}, u32[]{:S(2)}) collective-permute-start(bf16[192,768]{1,0:T(8,128)(2,1)S(1)} %collective-permute-done.122), channel_id=1, source_target_pairs={{0,4},{4,8},{8,12},{12,14},{14,10},{10,6},{6,2},{2,0},{1,5},{5,9},... | collective-permute-start | bytes 884744 | tf_op jit(solution)/shard_map/ppermute | solution.py:304
  581.8 27.7 %collective-permute-start.106 = (bf16[96,1536]{1,0:T(8,128)(2,1)S(1)}, bf16[96,1536]{1,0:T(8,128)(2,1)S(1)}, u32[]{:S(2)}, u32[]{:S(2)}) collective-permute-start(bf16[96,1536]{1,0:T(8,128)(2,1)S(1)} %collective-permute-done.105), channel_id=1, source_target_pairs={{4,0},{8,4},{12,8},{14,12},{10,14},{6,10},{2,6},{0,2},{5,1},{9,5},... | collective-permute-start | bytes 884744 | tf_op jit(solution)/shard_map/ppermute | solution.py:304
  (209 other events, 2195.2 us)

commit v3 on v2

v3 whole, which is shorter than its diff:
```python
import functools

import jax
import jax.numpy as jnp
from jax import lax
from jax.experimental import pallas as pl
from jax.experimental.pallas import tpu as pltpu
from jax.sharding import PartitionSpec as P

HEAD_DIM = 64
SYMBOLS = 24
SEQ = 160
PARTS = 3
RING = 8
BLOCK = 384
TAIL = 16
EPS = 1e-05
SCALE = HEAD_DIM**-0.5
VMEM_LIMIT = 14 * 1024 * 1024

root_half = 0.7071067811865476
root_two_pi = 0.3989422804014327
BF = jnp.bfloat16
F32 = jnp.float32


def swap(value):
    return lax.ppermute(value, "tensor", [(0, 1), (1, 0)])


def dot(a, b):
    return jnp.dot(a, b, preferred_element_type=F32)


def dot_rows(a, b):
    return lax.dot_general(a, b, (((1,), (1,)), ((), ())), preferred_element_type=F32)


def dot_cols(a, b):
    return lax.dot_general(a, b, (((0,), (0,)), ((), ())), preferred_element_type=F32)


def in_order(core, own, other):
    first = core == 0
    return jnp.concatenate(
        [jnp.where(first, own, other), jnp.where(first, other, own)], axis=1
    )


def own_part(core, value):
    half = value.shape[1] // 2
    return jnp.where(core == 0, value[:, :half], value[:, half:])


def normalise(rows):
    centred = rows - jnp.mean(rows, axis=-1, keepdims=True)
    inv_root = lax.rsqrt(jnp.mean(centred * centred, axis=-1, keepdims=True) + EPS)
    return centred * inv_root, inv_root


def norm_back(grads, normal, inv_root, gain):
    scaled = grads * gain
    inner = (
        scaled
        - jnp.mean(scaled, axis=-1, keepdims=True)
        - normal * jnp.mean(scaled * normal, axis=-1, keepdims=True)
    )
    return inner * inv_root


def pair_spans(width):
    return [slice(at, at + 2 * HEAD_DIM) for at in range(0, width, 2 * HEAD_DIM)]


def left_head():
    return lax.broadcasted_iota(jnp.int32, (1, 2 * HEAD_DIM), 1) < HEAD_DIM


def pair_scores(first, second):
    left = left_head().astype(BF)
    both = jnp.concatenate([first * left, first * (1 - left)], axis=0)
    return dot_rows(both, second).reshape(2, SEQ, SEQ)


def pair_product(matrices, block):
    found = dot(matrices.reshape(2 * SEQ, SEQ), block)
    return jnp.where(left_head(), found[:SEQ], found[SEQ:]).astype(BF)


def turned(matrices):
    return jnp.concatenate([matrices[0].T, matrices[1].T], axis=0)


def attn_forward_kernel(choose, keep, start, count, marks, *refs):
    refs = list(refs)
    own, other = refs.pop(0), refs.pop(0)
    if choose:
        own_late, other_late = refs.pop(0), refs.pop(0)
    joint, output = refs.pop(0), refs.pop(0)
    chain = pl.program_id(0)
    tag = marks[3 + start + chain]
    core = marks[1]
    a, b = own[...], other[...]
    if choose:
        early = marks[0] == 0
        a = jnp.where(early, a, own_late[...])
        b = jnp.where(early, b, other_late[...])
    rows = in_order(core, a, b)
    q, k, v = [dot(rows, joint[tag, j]).astype(BF) for j in range(3)]
    key_live = lax.broadcasted_iota(jnp.int32, (1, SEQ, 1), 1) < marks[3 + count + start + chain]
    spans = pair_spans(q.shape[1])
    scores = [pair_scores(k[:, s], q[:, s] * jnp.asarray(SCALE, BF)) for s in spans]
    probs = []
    for found in scores:
        found = jnp.where(key_live, found, -1000000000.0)
        shifted = jnp.exp(found - jnp.max(found, axis=1, keepdims=True))
        probs.append((shifted * (1.0 / jnp.sum(shifted, axis=1, keepdims=True))).astype(BF))
    mixed = jnp.concatenate(
        [pair_product(turned(p), v[:, s]) for p, s in zip(probs, spans)], axis=1
    )
    refs[0][...] = rows
    refs[1][...] = dot(mixed, output[tag]).astype(BF)
    if keep:
        refs[2][...] = jnp.concatenate([q, k, v], axis=1)
        for at, found in enumerate(probs):
            refs[3][0, 2 * at : 2 * at + 2] = found
        refs[4][...] = mixed


def feed_forward_kernel(keep, start, marks, rows, part, other, gains, shifts, up, bias, down, *outs):
    tag = marks[3 + start + pl.program_id(0)]
    total = rows[...].astype(F32) + (part[...].astype(F32) + other[...].astype(F32))
    normal, inv_root = normalise(total)
    low = (normal * gains[0:1] + shifts[0:1]).astype(BF)
    pre = dot(low, up[tag]) + jnp.where(tag == 0, bias[0:1], bias[1:2]).astype(F32)
    cdf = 0.5 * (1.0 + lax.erf(pre * root_half))
    hidden = (pre * cdf).astype(BF)
    outs[0][...] = dot(hidden, down[tag]).astype(BF)
    outs[1][...] = normal
    if keep:
        outs[2][...] = inv_root
        outs[3][...] = low
        outs[4][...] = hidden
        outs[5][...] = (cdf + pre * jnp.exp(-0.5 * pre * pre) * root_two_pi).astype(BF)


def second_norm(normal, part, other, gains, shifts):
    first = normal[...] * gains[0:1] + shifts[0:1]
    return normalise(first + (part[...].astype(F32) + other[...].astype(F32)))


def last_norm_kernel(marks, normal, part, other, gains, shifts, out):
    second, _ = second_norm(normal, part, other, gains, shifts)
    out[...] = own_part(marks[1], (second * gains[1:2] + shifts[1:2]).astype(BF))


def carry_over(carried, sums):
    @pl.when(pl.program_id(0) == 0)
    def _():
        sums[...] = carried[...]


def add_sums(grads, normal, carried, sums):
    carry_over(carried, sums)
    sums[0] += jnp.sum(grads * normal, axis=0, keepdims=True)
    sums[1] += jnp.sum(grads, axis=0, keepdims=True)


def feed_back_kernel(last, start, marks, *refs):
    refs = list(refs)
    normal, part, other, gains, shifts, own_cot, other_cot = refs[:7]
    refs = refs[7:]
    tag = marks[3 + start + pl.program_id(0)]
    core = marks[1]
    a, b = own_cot[...], other_cot[...]
    if last:
        late = marks[0] == 1
        a = jnp.where(late, a, refs.pop(0)[...])
        b = jnp.where(late, b, refs.pop(0)[...])
    slope, up, down = refs[:3]
    refs = refs[3:]
    if last:
        carried_sums, carried_bias = refs.pop(0), refs.pop(0)
    outs = refs
    grads = in_order(core, a, b).astype(F32)
    second, inv_root = second_norm(normal, part, other, gains, shifts)
    back = norm_back(grads, second, inv_root, gains[1:2])
    low = back.astype(BF)
    d_pre = (dot_rows(low, down[tag]) * slope[...].astype(F32)).astype(BF)
    outs[0][...] = back
    outs[1][...] = dot_rows(d_pre, up[tag]).astype(BF)
    if last:
        outs[2][...] = low
        outs[3][...] = d_pre
        outs[4][...] = own_part(core, (second * gains[1:2] + shifts[1:2]).astype(BF))
        add_sums(grads, second, carried_sums, outs[5])
        carry_over(carried_bias, outs[6])
        outs[6][tag] += jnp.sum(d_pre.astype(F32), axis=0, keepdims=True)


def attn_back_kernel(
    last, start, marks, back, part, other, normal, inv_root, gains, joined, probs, joint, output, *outs
):
    if last:
        carried, *outs = outs
    tag = marks[3 + start + pl.program_id(0)]
    core = marks[1]
    grads = back[...] + (part[...].astype(F32) + other[...].astype(F32))
    back_one = norm_back(grads, normal[...], inv_root[...], gains[0:1])
    low = back_one.astype(BF)
    d_mixed = dot_rows(low, output[tag]).astype(BF)
    width = d_mixed.shape[1]
    q, k, v = [joined[:, j * width : (j + 1) * width] for j in range(3)]
    spans = pair_spans(width)
    d_probs = [pair_scores(v[:, s], d_mixed[:, s]) for s in spans]
    held = [probs[0, 2 * at : 2 * at + 2] for at in range(len(spans))]
    d_scores = []
    for found, kept in zip(d_probs, held):
        wide = kept.astype(F32)
        inner = jnp.sum(wide * found, axis=1, keepdims=True)
        d_scores.append((wide * (found - inner)).astype(BF))
    scale = jnp.asarray(SCALE, BF)
    d_k = [pair_product(d, q[:, s]) * scale for d, s in zip(d_scores, spans)]
    d_v = [pair_product(h, d_mixed[:, s]) for h, s in zip(held, spans)]
    d_q = [pair_product(turned(d), k[:, s]) * scale for d, s in zip(d_scores, spans)]
    pieces = [d_q, d_k, d_v]
    blocks = [jnp.concatenate(p, axis=1) for p in pieces]
    d_rows = sum(dot_rows(blocks[j], joint[tag, j]) for j in range(3)).astype(BF)
    outs[0][...] = own_part(core, back_one) + own_part(core, d_rows).astype(F32)
    outs[1][...] = own_part(1 - core, d_rows)
    if last:
        outs[2][...] = low
        outs[3][...] = jnp.concatenate(blocks, axis=1)
        add_sums(grads, normal[...], carried, outs[4])


def behind(kernel, taken, ignored):
    def call(marks, *refs):
        kernel(marks, *refs[:taken], *refs[taken + ignored :])

    return call


ANY = pl.BlockSpec(memory_space=pl.ANY)
HBM = pl.BlockSpec(memory_space=pltpu.HBM)
TOKEN = jax.ShapeDtypeStruct((8, 128), F32)
TOKEN_BLOCK = pl.BlockSpec((8, 128), lambda *_: (0, 0))


def sign_off(token):
    token[...] = jnp.zeros_like(token)


class Order:
    def __init__(self):
        self.tokens = ()

    def run(self, call, *args):
        *results, token = call(*args, self.tokens)
        self.tokens = (token,)
        return results

    def after(self, value):
        return lax.optimization_barrier((value, *self.tokens))[0]


def run_chains(kernel, name, marks, chains, ins, outs, flops, after):
    specs = []
    for array, kind, first in ins:
        if kind == "rows":
            specs.append(
                pl.BlockSpec((SEQ, array.shape[1]), lambda i, *_, first=first: (first + i, 0))
            )
        elif kind == "chain":
            rest = array.shape[1:]
            specs.append(
                pl.BlockSpec(
                    (1,) + rest, lambda i, *_, first=first, n=len(rest): (first + i,) + (0,) * n
                )
            )
        else:
            specs.append(pl.BlockSpec(memory_space=pltpu.VMEM))
    shapes, out_specs = [], []
    for trailing, dtype, kind in outs:
        if kind == "rows":
            shapes.append(jax.ShapeDtypeStruct((chains * SEQ,) + trailing, dtype))
            out_specs.append(pl.BlockSpec((SEQ,) + trailing, lambda i, *_: (i, 0)))
        elif kind == "chain":
            shapes.append(jax.ShapeDtypeStruct((chains,) + trailing, dtype))
            out_specs.append(
                pl.BlockSpec((1,) + trailing, lambda i, *_, n=len(trailing): (i,) + (0,) * n)
            )
        else:
            shapes.append(jax.ShapeDtypeStruct(trailing, dtype))
            out_specs.append(pl.BlockSpec(trailing, lambda i, *_, n=len(trailing): (0,) * n))
    moved = sum(a.size * a.dtype.itemsize for a, _, _ in ins)
    specs += [ANY] * len(after)
    shapes.append(TOKEN)
    out_specs.append(TOKEN_BLOCK)

    def signing(marks, *refs):
        sign_off(refs[-1])
        kernel(marks, *refs[:-1])

    return pl.pallas_call(
        behind(signing, len(ins), len(after)),
        grid_spec=pltpu.PrefetchScalarGridSpec(
            num_scalar_prefetch=1, grid=(chains,), in_specs=specs, out_specs=out_specs
        ),
        out_shape=shapes,
        compiler_params=pltpu.CompilerParams(vmem_limit_bytes=VMEM_LIMIT),
        cost_estimate=pl.CostEstimate(
            flops=flops // 1000, bytes_accessed=moved // 1000, transcendentals=0
        ),
        name=name,
    )(marks, *[a for a, _, _ in ins], *after)


def ring_spot(marks, step, way):
    return lax.rem(marks[2] + 2 * RING + way * step, RING)


def span(at):
    return pl.ds(pl.multiple_of(at * BLOCK, BLOCK), BLOCK)


def cut(ref, at):
    return ref[:, span(at)]


def set_rows(marks, block, which):
    pieces = []
    for chain in range(block.shape[0] // SEQ):
        piece = block[chain * SEQ : (chain + 1) * SEQ]
        pieces.append(jnp.where(marks[3 + chain] == which, piece, jnp.zeros_like(piece)))
    return jnp.concatenate(pieces, axis=0)


def fetch(lists, scratch, sems):
    @pl.when(pl.program_id(0) == 0)
    def _():
        copies = []
        for refs, held in zip(lists, scratch):
            rows = held.shape[0] // len(refs)
            for at, ref in enumerate(refs):
                copies.append(
                    pltpu.make_async_copy(
                        ref, held.at[at * rows : (at + 1) * rows], sems.at[len(copies)]
                    )
                )
        for copy in copies:
            copy.start()
        for copy in copies:
            copy.wait()


def feed_shard(marks, which, hidden, d_down, low, d_pre):
    return (
        dot_cols(set_rows(marks, hidden, which), d_down).astype(BF),
        dot_cols(set_rows(marks, low, which), d_pre).astype(BF),
    )


def first_shard_kernel(parts, marks, *refs):
    out, token = refs[8 * parts :]
    sign_off(token)
    for which in range(2):
        blocks = []
        for n in range(4):
            at = (4 * which + n) * parts
            blocks.append(jnp.concatenate([ref[...] for ref in refs[at : at + parts]], axis=0))
        out[which, :BLOCK], out[which, BLOCK:] = feed_shard(marks, which, *blocks)


def run_first_shard(marks, lists, after):
    specs, ins = [], []
    for way in (-1, 1):
        for n, arrays in enumerate(lists):
            for array in arrays:

                def index(i, marks, n=n, way=way):
                    spot = ring_spot(marks, 1, way)
                    return 0, (lax.div(spot, 2) if n in (0, 3) else lax.rem(spot, 2))

                specs.append(pl.BlockSpec((array.shape[0], BLOCK), index))
                ins.append(array)
    shape = (2, 2 * BLOCK, BLOCK)
    return pl.pallas_call(
        behind(functools.partial(first_shard_kernel, len(lists[0])), len(ins), len(after)),
        grid_spec=pltpu.PrefetchScalarGridSpec(
            num_scalar_prefetch=1,
            grid=(1,),
            in_specs=specs + [ANY] * len(after),
            out_specs=[pl.BlockSpec(shape, lambda i, *_: (0, 0, 0)), TOKEN_BLOCK],
        ),
        out_shape=[jax.ShapeDtypeStruct(shape, BF), TOKEN],
        compiler_params=pltpu.CompilerParams(vmem_limit_bytes=20 * 1024 * 1024),
        name="first_shard",
    )(marks, *ins, *after)


def feed_weights_kernel(first, parts, marks, *refs):
    out, token, hidden, d_down, low, d_pre, sems = refs[4 * parts :]
    sign_off(token)
    fetch([refs[n * parts : (n + 1) * parts] for n in range(4)], refs[4 * parts + 2 : -1], sems)
    step = first + pl.program_id(0) + 1
    for which, way in ((0, -1), (1, 1)):
        spot = ring_spot(marks, step, way)
        far, near = lax.div(spot, 2), lax.rem(spot, 2)
        out[0, which, :BLOCK], out[0, which, BLOCK:] = feed_shard(
            marks, which, cut(hidden, far), cut(d_down, near), cut(low, near), cut(d_pre, far)
        )


def two_halves(value):
    high = value.astype(BF).astype(F32)
    return jnp.concatenate([high, value - high], axis=0).astype(BF)


def one_whole(rows):
    rows = rows.astype(F32)
    return rows[: TAIL // 2] + rows[TAIL // 2 :]


def count_rows(live, predicted, targets):
    symbols = lax.broadcasted_iota(jnp.int32, (128, live.shape[1]), 0)
    hits = (targets[...] == symbols) & (live[...] > 0)
    right = hits & (predicted[...] == targets[...])
    ones = jnp.ones((8, live.shape[1]), BF)
    found = [dot_rows(ones, h.astype(F32).astype(BF)) for h in (hits, right)]
    return jnp.concatenate(found + [jnp.zeros_like(found[0])], axis=1)[0:1]


def attn_weights_kernel(first, parts, marks, *refs):
    bias, *sums, live, predicted, targets, out, token = refs[4 * parts : -5]
    rows, d_joined, mixed, d_attn, sems = refs[-5:]
    fetch([refs[n * parts : (n + 1) * parts] for n in range(4)], refs[-5:-1], sems)
    sign_off(token)
    step = first + pl.program_id(0) + 1
    for which, way in ((0, -1), (1, 1)):
        spot = ring_spot(marks, step, way)
        far, near = lax.div(spot, 2), lax.rem(spot, 2)

        @pl.when(far < 3)
        def _():
            out[0, which, :BLOCK] = dot_cols(
                set_rows(marks, cut(rows, near), which), cut(d_joined, far)
            ).astype(BF)

        @pl.when(far == 3)
        def _():
            out[0, which, :BLOCK] = dot_cols(
                set_rows(marks, mixed[...], which), cut(d_attn, near)
            ).astype(BF)

        early = far < 2
        small = jnp.where(
            early,
            bias[which, :, span(jnp.where(early, spot, 0))],
            sums[which][jnp.where(early, 0, far - 2), :, span(near)],
        )
        place = lax.broadcasted_iota(jnp.int32, (TAIL // 2, BLOCK), 0)
        small = jnp.where(place == 0, small, 0.0)
        out[0, which, BLOCK:] = two_halves(small)
        if which == 0:

            @pl.when(spot == 0)
            def _():
                counts = count_rows(live, predicted, targets)
                out[0, which, BLOCK:] = two_halves(jnp.where(place == 1, counts, small))


def run_weights(kernel, name, marks, first, steps, lists, rest, rows_out, after):
    ins = [a for arrays in lists for a in arrays] + list(rest)
    shape = (2, rows_out, BLOCK)
    return pl.pallas_call(
        behind(functools.partial(kernel, first, len(lists[0])), len(ins), len(after)),
        grid_spec=pltpu.PrefetchScalarGridSpec(
            num_scalar_prefetch=1,
            grid=(steps,),
            in_specs=[HBM] * (len(ins) - len(rest))
            + [pl.BlockSpec(memory_space=pltpu.VMEM)] * len(rest)
            + [ANY] * len(after),
            out_specs=[pl.BlockSpec((1,) + shape, lambda i, *_: (i, 0, 0, 0)), TOKEN_BLOCK],
            scratch_shapes=[
                pltpu.VMEM((sum(a.shape[0] for a in arrays), arrays[0].shape[1]), BF)
                for arrays in lists
            ]
            + [pltpu.SemaphoreType.DMA((len(ins) - len(rest),))],
        ),
        out_shape=[jax.ShapeDtypeStruct((steps,) + shape, BF), TOKEN],
        compiler_params=pltpu.CompilerParams(vmem_limit_bytes=20 * 1024 * 1024),
        cost_estimate=pl.CostEstimate(
            flops=steps * 4 * rows_out * BLOCK,
            bytes_accessed=steps * rows_out,
            transcendentals=0,
        ),
        name=name,
    )(marks, *ins, *after)


def add_kernel(tail, ahead, back, local, out_ahead, out_back, token):
    sign_off(token)
    for which, (ref, out) in enumerate(((ahead, out_ahead), (back, out_back))):
        total = ref[...].astype(F32) + local[0, which].astype(F32)
        out[...] = total.astype(BF)
        if tail:
            out[tail:] = two_halves(one_whole(total[tail:]))


def add_step(pair, local, at, after):
    shape = local.shape[2:]
    block = pl.BlockSpec(shape, lambda i: (0, 0))

    tail = BLOCK if shape[0] == BLOCK + TAIL else 0

    def call(*refs):
        add_kernel(tail, *refs[:3], *refs[3 + len(after) :])

    return pl.pallas_call(
        call,
        grid=(1,),
        in_specs=[block, block, pl.BlockSpec((1, 2) + shape, lambda i: (at, 0, 0, 0))]
        + [ANY] * len(after),
        out_specs=[block, block, TOKEN_BLOCK],
        out_shape=[jax.ShapeDtypeStruct(shape, BF)] * 2 + [TOKEN],
        compiler_params=pltpu.CompilerParams(vmem_limit_bytes=VMEM_LIMIT),
        cost_estimate=pl.CostEstimate(
            flops=2 * shape[0] * shape[1],
            bytes_accessed=12 * shape[0] * shape[1],
            transcendentals=0,
        ),
        name="ring_add",
    )(*pair, local, *after)


def feed_place_kernel(step, marks, ahead, back, outs, wide, sems):
    down, up = outs
    copies = []
    for which, (ref, way) in enumerate(((ahead, -1), (back, 1))):
        spot = ring_spot(marks, step, way)
        far, near = lax.div(spot, 2), lax.rem(spot, 2)
        wide[which] = ref[...].astype(F32)
        copies += [
            pltpu.make_async_copy(
                wide.at[which, :BLOCK], down.at[which, span(far), span(near)], sems.at[2 * which]
            ),
            pltpu.make_async_copy(
                wide.at[which, BLOCK:], up.at[which, span(near), span(far)], sems.at[2 * which + 1]
            ),
        ]
        for copy in copies[-2:]:
            copy.start()
    for copy in copies:
        copy.wait()


def attn_place_kernel(step, marks, ahead, back, outs, wide, sems):
    joint, output, small = outs
    copies = []
    for which, (ref, way) in enumerate(((ahead, -1), (back, 1))):
        spot = ring_spot(marks, step, way)
        far, near = lax.div(spot, 2), lax.rem(spot, 2)
        wide[which] = ref[...].astype(F32)
        wide[which, BLOCK : BLOCK + TAIL // 2] = one_whole(ref[BLOCK:])
        copy = pltpu.make_async_copy(
            wide.at[which, BLOCK : BLOCK + TAIL // 2], small.at[which, spot], sems.at[2 + which]
        )
        copy.start()
        copies.append(copy)

        @pl.when(far < 3)
        def _():
            copy = pltpu.make_async_copy(
                wide.at[which, :BLOCK], joint.at[which, far, span(near)], sems.at[which]
            )
            copy.start()
            copy.wait()

        @pl.when(far == 3)
        def _():
            copy = pltpu.make_async_copy(
                wide.at[which, :BLOCK], output.at[which, :, span(near)], sems.at[which]
            )
            copy.start()
            copy.wait()

    for copy in copies:
        copy.wait()


def place_step(kernel, name, marks, step, pair, held, after):
    shape = pair[0].shape
    block = pl.BlockSpec(shape, lambda i, *_: (0, 0))

    count = len(held)

    def call(marks, ahead, back, *refs):
        refs = refs[count + len(after) :]
        sign_off(refs[count])
        kernel(step, marks, ahead, back, refs[:count], *refs[count + 1 :])

    return pl.pallas_call(
        call,
        grid_spec=pltpu.PrefetchScalarGridSpec(
            num_scalar_prefetch=1,
            grid=(1,),
            in_specs=[block, block] + [HBM] * count + [ANY] * len(after),
            out_specs=[HBM] * count + [TOKEN_BLOCK],
            scratch_shapes=[pltpu.VMEM((2,) + shape, F32), pltpu.SemaphoreType.DMA((4,))],
        ),
        out_shape=[jax.ShapeDtypeStruct(h.shape, h.dtype) for h in held] + [TOKEN],
        input_output_aliases={3 + i: i for i in range(count)},
        compiler_params=pltpu.CompilerParams(vmem_limit_bytes=VMEM_LIMIT),
        cost_estimate=pl.CostEstimate(
            flops=0, bytes_accessed=12 * shape[0] * shape[1], transcendentals=0
        ),
        name=name,
    )(marks, *pair, *held, *after)


def unwritten(*shapes):
    return pl.pallas_call(
        lambda *refs: None,
        out_specs=[HBM] * len(shapes),
        out_shape=[jax.ShapeDtypeStruct(s, F32) for s in shapes],
        compiler_params=pltpu.CompilerParams(vmem_limit_bytes=1024 * 1024),
        name="unwritten",
    )()


class Ring:
    def __init__(self):
        self.count = lax.axis_size("dp")
        assert self.count % RING == 0
        order = list(range(0, RING, 2)) + list(range(1, RING, 2))[::-1]
        rank = lax.rem(lax.axis_index("dp"), RING)
        self.place = jnp.zeros((), jnp.int32)
        for at, member in enumerate(order):
            self.place = jnp.where(rank == member, at, self.place)
        self.ahead = [
            (base + order[i], base + order[(i + 1) % RING])
            for base in range(0, self.count, RING)
            for i in range(RING)
        ]
        self.back = [(b, a) for a, b in self.ahead]

    def send(self, pair):
        return lax.ppermute(pair[0], "dp", self.ahead), lax.ppermute(pair[1], "dp", self.back)

    def across(self, pair):
        result = []
        for value in pair:
            total = value.astype(F32)
            moving = value
            for _ in range(self.count // RING - 1):
                pairs = [(i, (i + RING) % self.count) for i in range(self.count)]
                moving = lax.ppermute(moving, "dp", pairs)
                total = total + moving.astype(F32)
            low = total.astype(BF)
            if total.shape[0] == BLOCK + TAIL and self.count > RING:
                tail = two_halves(one_whole(total[BLOCK:]))
                low = jnp.concatenate([low[:BLOCK], tail], axis=0)
            result.append(low)
        return result


def shards(
    chain_inputs,
    cotangent,
    chain_tags,
    pad_mask,
    predicted,
    target_ids,
    joint_proj,
    output_proj,
    up_proj,
    up_bias,
    down_proj,
    norm_gain,
    norm_shift,
):
    section = lax.axis_index("section")
    core = lax.axis_index("tensor")
    tokens, half = chain_inputs.shape
    width = 2 * half
    all_chains = tokens // SEQ
    chains = all_chains // PARTS
    tags = (chain_tags > 0).astype(jnp.int32)
    ring = Ring()
    chain_of = jnp.arange(tokens, dtype=jnp.int32)[None] // SEQ
    belongs = chain_of == jnp.arange(all_chains, dtype=jnp.int32)[:, None]
    lengths = jnp.sum(jnp.where(belongs, pad_mask[None], 0), axis=1)
    marks = jnp.concatenate([jnp.stack([section, core, ring.place]).astype(jnp.int32), tags, lengths])
    small = [ids.reshape(1, tokens) for ids in (pad_mask, predicted, target_ids)]
    joint = joint_proj[0].transpose(0, 2, 1, 3)
    output, up, bias, down = output_proj[0], up_proj[0], up_bias[0], down_proj[0]
    gains, shifts = norm_gain[0], norm_shift[0]
    units = up.shape[2]
    local = output.shape[1]
    heads = local // HEAD_DIM
    rows = chains * SEQ
    attn_flops = 2 * rows * (width * 4 * local + 2 * local * SEQ)
    feed_flops = 2 * rows * width * 2 * units

    cot_other = swap(cotangent)
    rows_other = swap(chain_inputs)

    order = Order()

    def attn_forward(p, late, keep):
        start = p * chains
        ins = [(chain_inputs, "rows", start), (rows_other, "rows", start)]
        if late is not None:
            ins += [(late[0], "rows", 0), (late[1], "rows", 0)]
        ins += [(joint, "whole", 0), (output, "whole", 0)]
        outs = [((width,), BF, "rows"), ((width,), BF, "rows")]
        if keep:
            outs += [
                ((3 * local,), BF, "rows"),
                ((heads, SEQ, SEQ), BF, "chain"),
                ((local,), BF, "rows"),
            ]
        kernel = functools.partial(
            attn_forward_kernel, late is not None, keep, start, all_chains
        )
        found = order.run(
            run_chains, kernel, "attn_forward", marks, chains, ins, outs, attn_flops
        )
        names = ("rows", "part", "joined", "probs", "mixed")
        kept = dict(zip(names, found))
        kept["part_other"] = swap(kept["part"])
        return kept

    def feed_forward(p, kept, keep):
        ins = [(kept[n], "rows", 0) for n in ("rows", "part", "part_other")]
        ins += [(a, "whole", 0) for a in (gains, shifts, up, bias, down)]
        outs = [((width,), BF, "rows"), ((width,), F32, "rows")]
        if keep:
            outs += [
                ((1,), F32, "rows"),
                ((width,), BF, "rows"),
                ((units,), BF, "rows"),
                ((units,), BF, "rows"),
            ]
        kernel = functools.partial(feed_forward_kernel, keep, p * chains)
        found = order.run(
            run_chains, kernel, "feed_forward", marks, chains, ins, outs, feed_flops
        )
        names = ("down", "normal", "inv_root", "low", "hidden", "slope")
        kept.update(zip(names, found))
        kept["down_other"] = swap(kept["down"])

    def last_norm(p, kept):
        ins = [(kept[n], "rows", 0) for n in ("normal", "down", "down_other")]
        ins += [(gains, "whole", 0), (shifts, "whole", 0)]
        outs = [((half,), BF, "rows")]
        found = order.run(
            run_chains, last_norm_kernel, "last_norm", marks, chains, ins, outs, 0
        )
        return lax.ppermute(found[0], "section", [(0, 1), (1, 0)])

    def feed_back(p, kept, late, carried=None):
        ins = [(kept[n], "rows", 0) for n in ("normal", "down", "down_other")]
        ins += [(gains, "whole", 0), (shifts, "whole", 0)]
        ins += [(cotangent, "rows", p * chains), (cot_other, "rows", p * chains)]
        if late is not None:
            ins += [(late[0], "rows", 0), (late[1], "rows", 0)]
        ins += [(kept["slope"], "rows", 0), (up, "whole", 0), (down, "whole", 0)]
        if late is not None:
            ins += [(carried["sums"], "whole", 0), (carried["bias"], "whole", 0)]
        outs = [((width,), F32, "rows"), ((width,), BF, "rows")]
        if late is not None:
            outs += [
                ((width,), BF, "rows"),
                ((units,), BF, "rows"),
                ((half,), BF, "rows"),
                ((2, 1, width), F32, "whole"),
                ((2, 1, units), F32, "whole"),
            ]
        kernel = functools.partial(feed_back_kernel, late is not None, p * chains)
        found = order.run(
            run_chains, kernel, "feed_back", marks, chains, ins, outs, feed_flops
        )
        names = ("back", "part", "d_down", "d_pre", "outputs", "sums", "bias")
        found = dict(zip(names, found))
        found["part_other"] = swap(found["part"])
        return found

    def attn_back(p, kept, feed, last, carried=None):
        ins = [(feed[n], "rows", 0) for n in ("back", "part", "part_other")]
        ins += [(kept["normal"], "rows", 0), (kept["inv_root"], "rows", 0), (gains, "whole", 0)]
        ins += [(kept["joined"], "rows", 0), (kept["probs"], "chain", 0)]
        ins += [(joint, "whole", 0), (output, "whole", 0)]
        if last:
            ins.append((carried["sums"], "whole", 0))
        outs = [((half,), F32, "rows"), ((half,), BF, "rows")]
        if last:
            outs += [
                ((width,), BF, "rows"),
                ((3 * local,), BF, "rows"),
                ((2, 1, width), F32, "whole"),
            ]
        kernel = functools.partial(attn_back_kernel, last, p * chains)
        found = order.run(
            run_chains, kernel, "attn_back", marks, chains, ins, outs, attn_flops
        )
        names = ("mine", "theirs", "d_attn", "d_joined", "sums")
        found = dict(zip(names, found))
        found["grads"] = found["mine"] + swap(found["theirs"]).astype(F32)
        return found

    early, sent, late, kept = {}, {}, {}, {}

    def start_early(p):
        early[p] = attn_forward(p, None, False)

    def feed_early(p):
        feed_forward(p, early[p], False)

    def norm_early(p):
        sent[p] = last_norm(p, early[p])

    def receive(p):
        moved = order.after(sent[p])
        late[p] = (moved, swap(moved))

    def start_kept(p):
        kept[p] = attn_forward(p, late[p], True)

    def feed_kept(p):
        feed_forward(p, kept[p], True)

    first_feed, first_attn, sent_back, late_back = {}, {}, {}, {}
    no_sums = jnp.zeros((2, 1, width), F32)
    feed = {-1: dict(sums=no_sums, bias=jnp.zeros((2, 1, units), F32))}
    attn = {-1: dict(sums=no_sums)}

    def feed_first(p):
        first_feed[p] = feed_back(p, kept[p], None)

    def attn_first(p):
        first_attn[p] = attn_back(p, kept[p], first_feed[p], False)
        total = first_attn[p]["grads"].astype(BF)
        sent_back[p] = lax.ppermute(total, "section", [(1, 0), (0, 1)])

    def receive_back(p):
        moved = order.after(sent_back[p])
        late_back[p] = (moved, swap(moved))

    def feed_last(p):
        feed[p] = feed_back(p, kept[p], late_back[p], feed[p - 1])

    def attn_last(p):
        attn[p] = attn_back(p, kept[p], feed[p], True, attn[p - 1])

    for step, p in (
        (start_early, 0),
        (start_early, 1),
        (feed_early, 0),
        (start_early, 2),
        (norm_early, 0),
        (feed_early, 1),
        (norm_early, 1),
        (receive, 0),
        (feed_early, 2),
        (norm_early, 2),
        (receive, 1),
        (start_kept, 0),
        (start_kept, 1),
        (receive, 2),
        (feed_kept, 0),
        (start_kept, 2),
        (feed_kept, 1),
        (feed_kept, 2),
        (feed_first, 0),
        (feed_first, 1),
        (attn_first, 0),
        (feed_first, 2),
        (attn_first, 1),
        (receive_back, 0),
        (attn_first, 2),
        (feed_last, 0),
        (receive_back, 1),
        (feed_last, 1),
        (receive_back, 2),
        (feed_last, 2),
    ):
        step(p)
    parts = range(PARTS)
    feed_lists = [
        [kept[p]["hidden"] for p in parts],
        [feed[p]["d_down"] for p in parts],
        [kept[p]["low"] for p in parts],
        [feed[p]["d_pre"] for p in parts],
    ]

    def feed_weights(first, steps):
        return order.run(
            run_weights,
            feed_weights_kernel,
            "feed_weights",
            marks,
            first,
            steps,
            feed_lists,
            [],
            2 * BLOCK,
        )[0]

    def add_local(pair, local, at):
        return order.run(add_step, pair, local, at)

    first_shards = order.run(run_first_shard, marks, feed_lists)[0]
    feed_pair = ring.send((first_shards[0], first_shards[1]))
    feed_local = feed_weights(1, RING - 1)
    feed_pair = ring.send(add_local(feed_pair, feed_local, 0))
    attn_last(0)
    attn_last(1)
    feed_pair = ring.send(add_local(feed_pair, feed_local, 1))
    attn_last(2)
    attn_lists = [
        [kept[p]["rows"] for p in parts],
        [attn[p]["d_joined"] for p in parts],
        [kept[p]["mixed"] for p in parts],
        [attn[p]["d_attn"] for p in parts],
    ]

    small = [feed[PARTS - 1]["bias"], attn[PARTS - 1]["sums"], feed[PARTS - 1]["sums"], *small]

    def attn_weights(first, steps):
        return order.run(
            run_weights,
            attn_weights_kernel,
            "attn_weights",
            marks,
            first,
            steps,
            attn_lists,
            small,
            BLOCK + TAIL,
        )[0]

    first_shards = attn_weights(0, 1)
    attn_pair = ring.send((first_shards[0, 0], first_shards[0, 1]))
    feed_pair = ring.send(add_local(feed_pair, feed_local, 2))
    attn_local = attn_weights(1, RING - 1)
    streams = [
        dict(
            pair=attn_pair,
            local=attn_local,
            sent=1,
            kernel=attn_place_kernel,
            name="attn_place",
            held=unwritten((2, 3, width, local), (2, local, width), (2, RING, 8, BLOCK)),
        ),
        dict(
            pair=feed_pair,
            local=feed_local,
            sent=4,
            kernel=feed_place_kernel,
            name="feed_place",
            held=unwritten((2, units, width), (2, width, units)),
        ),
    ]

    def turn(stream):
        sent = stream["sent"]
        *pair, token = lax.optimization_barrier((*stream["pair"], *order.tokens))
        order.tokens = (token,)
        if sent < RING:
            pair = add_local(pair, stream["local"], sent - 1)
            if sent == RING - 1:
                pair = ring.across(pair)
        stream["pair"] = ring.send(pair) if sent < 2 * RING - 2 else None
        if sent >= RING - 1:
            stream["held"] = order.run(
                place_step,
                stream["kernel"],
                stream["name"],
                marks,
                sent - RING + 1,
                pair,
                stream["held"],
            )
        stream["sent"] += 1

    attn_stream, feed_stream = streams
    while attn_stream["pair"] is not None or feed_stream["pair"] is not None:
        if attn_stream["pair"] is not None:
            turn(attn_stream)
        if attn_stream["sent"] < feed_stream["sent"]:
            turn(attn_stream)
        if feed_stream["pair"] is not None:
            turn(feed_stream)
    joint_out, output_out, small_out = attn_stream["held"]
    down_out, up_out = feed_stream["held"]

    def whole(pieces):
        return jnp.concatenate(pieces, axis=0)

    input_grads = whole([attn[p]["grads"] for p in parts])
    rows = small_out[:, :, 0]
    bias_grad = rows[:, :4].reshape(2, units)
    sums = rows[:, 4:].reshape(2, 2, width)
    counts = small_out[0, 0, 1].reshape(3, 128)[:2, :SYMBOLS]
    return (
        whole([feed[p]["outputs"] for p in parts])[None],
        input_grads[None],
        joint_out.transpose(0, 2, 1, 3)[None],
        output_out[None],
        up_out[None],
        bias_grad[None],
        down_out[None],
        sums[:, 0][None],
        sums[:, 1][None],
        counts.astype(jnp.int32),
    )


def solution(mesh):
    return jax.shard_map(
        shards,
        mesh=mesh,
        in_specs=(
            P("dp", "tensor"),
            P("dp", "tensor"),
            P("dp"),
            P("dp"),
            P("dp"),
            P("dp"),
            P("section", None, None, None, "tensor"),
            P("section", None, "tensor", None),
            P("section", None, None, "tensor"),
            P("section", None, "tensor"),
            P("section", None, "tensor", None),
            P("section", None, None),
            P("section", None, None),
        ),
        out_specs=(
            P("section", "dp", "tensor"),
            P("section", "dp", "tensor"),
            P("section", None, None, None, "tensor"),
            P("section", None, "tensor", None),
            P("section", None, None, "tensor"),
            P("section", None, "tensor"),
            P("section", None, "tensor", None),
            P("section", None, None),
            P("section", None, None),
            P(),
        ),
        check_vma=False,
    )
```

time: 658 us -> 436 us (0.66)
  starting transfers between devices: 141 us -> 74.4 us
  waiting for transfers between devices: 219 us -> 157 us
  local copies, waits for them, and re-layouts: 69.1 us -> 9.65 us
  other arithmetic: 50.7 us -> 4.53 us
  Pallas kernels: 141 us -> 180 us
  matrix products: 27 us -> 0 us
    ppermute x119 -> x62, starting transfers between devices: 135 us -> 66.7 us  [the longest x28 37.8 us: send(): lax.ppermute(pair[0], 'dp', self.ahead)]
    ppermute x119 -> x62, waiting for transfers between devices: 219 us -> 151 us  [the longest x28 125 us: send(): lax.ppermute(pair[0], 'dp', self.ahead)]
    pallas_call x18 -> x63, Pallas kernels: 141 us -> 180 us  [the longest x27 101 us: run_chains(): pl.pallas_call(behind(signing, len(ins), len(after)), grid_spec=pltpu.Pre...]
    unnamed x194 -> x89, local copies, waits for them, and re-layouts: 40.5 us -> 8.08 us
    dot_general x8 -> x0, matrix products: 27 us -> none  [dot_cols(): lax.dot_general(a, b, (((0,), (0,)), ((), ())), preferred_element_type=F32)]
    convert_element_type x51 -> x4, other arithmetic: 24.8 us -> 0.83 us  [the longest x1 0.66 us: shards(): tags = (chain_tags > 0).astype(jnp.int32)]
    broadcast_in_dim x4 -> x1, other arithmetic: 12.4 us -> 0.94 us  [shards(): whole([feed[p]['outputs'] for p in parts])[None]]
    dynamic_slice x8 -> x0, local copies, waits for them, and re-layouts: 7.68 us -> none  [shard(): lax.dynamic_slice_in_dim(whole, lax.rem(index, count) * rows, rows, 0)]
  transfers between devices with their start and end apart: 141 -> 94, of which waited for: 63 -> 40; matrix products, arithmetic and copies ran while one was open for 13% -> 1% of each run, Pallas kernels for 19% -> 36%
where the time goes in v3:
time: 436 us; the launch traced here: 428 us
  Pallas kernels  180 us (41%)
  waiting for transfers between devices  157 us (36%)
  starting transfers between devices  74.4 us (17%)
  local copies, waits for them, and re-layouts  9.65 us (2%)
  other arithmetic  4.53 us (1%)
    ppermute x28, waiting for transfers between devices, send(): lax.ppermute(pair[0], 'dp', self.ahead)  125 us
    pallas_call x27, Pallas kernels, run_chains(): pl.pallas_call(behind(signing, len(ins), len(after)), grid_spec=pltpu.Pre...  101 us
    pallas_call x3, Pallas kernels, run_weights(): pl.pallas_call(behind(functools.partial(kernel, first, len(lists[0])), le...  38.3 us
    ppermute x28, starting transfers between devices, send(): lax.ppermute(pair[0], 'dp', self.ahead)  37.8 us
    pallas_call x16, Pallas kernels, place_step(): pl.pallas_call(call, grid_spec=pltpu.PrefetchScalarGridSpec(num_scalar_pr...  35.6 us
    ppermute x28, starting transfers between devices, send(): lax.ppermute(pair[1], 'dp', self.back)  19.9 us
    ppermute x28, waiting for transfers between devices, send(): lax.ppermute(pair[1], 'dp', self.back)  15.8 us
  transfers between devices with their start and end apart: 94, of which 40 were waited for; matrix products, arithmetic and copies ran while one was open for 1% of the time, Pallas kernels for 36%

profile of v3, /device:TPU:0, one launch (start us, length us, event | category | flops | bytes accessed | tf_op | source)
XLA Modules:
  0.0 427.9 jit_solution(3366131907512045456)
XLA Ops:
  36.2 6.7 %collective-permute-done.3.refs_2_ = bf16[320,384]{1,0:T(8,128)(2,1)S(1)} collective-permute-done((bf16[320,384]{1,0:T(8,128)(2,1)S(1)}, bf16[320,384]{1,0:T(8,128)(2,1)S(1)}, u32[]{:S(2)}, u32[]{:S(2)}) %collective-permute-start.3) | collective-permute-done | bytes 245792 | tf_op jit(solution)/shard_map/ppermute | solution.py:761
  80.5 4.6 %attn_back.6 = (f32[320,384]{1,0:T(8,128)S(1)}, bf16[320,384]{1,0:T(8,128)(2,1)S(1)}, f32[8,128]{1,0:T(8,128)S(1)}) custom-call(s32[15]{0:T(128)S(1)} %concatenate.9.marks, f32[320,768]{1,0:T(8,128)S(1)} %get-tuple-element.366.refs_0_, bf16[320,768]{1,0:T(8,128)(2,1)S(1)} %get-tuple-element.367.refs_1_, ...), custom_call_target="tpu_custom_call" | custom-call | flops 833617 | bytes 9026 | tf_op jit(solution)/shard_map/attn_back/pallas_call | solution.py:305
  92.1 4.7 %attn_back.7 = (f32[320,384]{1,0:T(8,128)S(1)}, bf16[320,384]{1,0:T(8,128)(2,1)S(1)}, f32[8,128]{1,0:T(8,128)S(1)}) custom-call(s32[15]{0:T(128)S(1)} %concatenate.9.marks, f32[320,768]{1,0:T(8,128)S(1)} %get-tuple-element.378.refs_0_, bf16[320,768]{1,0:T(8,128)(2,1)S(1)} %get-tuple-element.379.refs_1_, ...), custom_call_target="tpu_custom_call" | custom-call | flops 833617 | bytes 9026 | tf_op jit(solution)/shard_map/attn_back/pallas_call | solution.py:305
  105.0 5.1 %feed_back.9 = (f32[320,768]{1,0:T(8,128)S(1)}, bf16[320,768]{1,0:T(8,128)(2,1)S(1)}, bf16[320,768]{1,0:T(8,128)(2,1)S(1)}, bf16[320,1536]{1,0:T(8,128)(2,1)S(1)...) custom-call(s32[15]{0:T(128)S(1)} %concatenate.9.marks, ...), custom_call_target="tpu_custom_call" | custom-call | flops 1509949 | bytes 14383 | tf_op jit(solution)/shard_map/feed_back/pallas_call | solution.py:305
  112.4 5.1 %feed_back.10 = (f32[320,768]{1,0:T(8,128)S(1)}, bf16[320,768]{1,0:T(8,128)(2,1)S(1)}, bf16[320,768]{1,0:T(8,128)(2,1)S(1)}, bf16[320,1536]{1,0:T(8,128)(2,1)S(1...) custom-call(s32[15]{0:T(128)S(1)} %concatenate.9.marks, ...), custom_call_target="tpu_custom_call" | custom-call | flops 1509949 | bytes 14383 | tf_op jit(solution)/shard_map/feed_back/pallas_call | solution.py:305
  120.9 5.1 %feed_back.11 = (f32[320,768]{1,0:T(8,128)S(1)}, bf16[320,768]{1,0:T(8,128)(2,1)S(1)}, bf16[320,768]{1,0:T(8,128)(2,1)S(1)}, bf16[320,1536]{1,0:T(8,128)(2,1)S(1...) custom-call(s32[15]{0:T(128)S(1)} %concatenate.9.marks, ...), custom_call_target="tpu_custom_call" | custom-call | flops 1509949 | bytes 14383 | tf_op jit(solution)/shard_map/feed_back/pallas_call | solution.py:305
  132.4 17.9 %feed_weights.1 = (bf16[7,2,768,384]{3,2,1,0:T(8,128)(2,1)S(1)}, f32[8,128]{1,0:T(8,128)S(1)}) custom-call(s32[15]{0:T(128)S(1)} %concatenate.9.marks, bf16[320,1536]{1,0:T(8,128)(2,1)S(1)} %get-tuple-element.413.refs_0_.refs_12_, bf16[320,1536]{1,0:T(8,128)(2,1)S(1)} %get-tuple-element.414.refs_1_.refs_13_, ...), custom_call_target="tpu_custom_call" | custom-call | flops 8257536 | bytes 5376 | tf_op jit(solution)/shard_map/feed_weights/pallas_call | solution.py:476
  154.6 4.8 %attn_back.9 = (f32[320,384]{1,0:T(8,128)S(1)}, bf16[320,384]{1,0:T(8,128)(2,1)S(1)}, bf16[320,768]{1,0:T(8,128)(2,1)S(1)}, bf16[320,1152]{1,0:T(8,128)(2,1)S(1)...) custom-call(s32[15]{0:T(128)S(1)} %concatenate.9.marks, f32[320,768]{1,0:T(8,128)S(1)} %copy-done.17, ...), custom_call_target="tpu_custom_call" | custom-call | flops 833617 | bytes 9032 | tf_op jit(solution)/shard_map/attn_back/pallas_call | solution.py:305
  159.5 4.8 %attn_back.10 = (f32[320,384]{1,0:T(8,128)S(1)}, bf16[320,384]{1,0:T(8,128)(2,1)S(1)}, bf16[320,768]{1,0:T(8,128)(2,1)S(1)}, bf16[320,1152]{1,0:T(8,128)(2,1)S(1...) custom-call(s32[15]{0:T(128)S(1)} %concatenate.9.marks, f32[320,768]{1,0:T(8,128)S(1)} %copy-done.21, ...), custom_call_target="tpu_custom_call" | custom-call | flops 833617 | bytes 9032 | tf_op jit(solution)/shard_map/attn_back/pallas_call | solution.py:305
  169.3 4.8 %attn_back.11 = (f32[320,384]{1,0:T(8,128)S(1)}, bf16[320,384]{1,0:T(8,128)(2,1)S(1)}, bf16[320,768]{1,0:T(8,128)(2,1)S(1)}, bf16[320,1152]{1,0:T(8,128)(2,1)S(1...) custom-call(s32[15]{0:T(128)S(1)} %concatenate.9.marks, f32[320,768]{1,0:T(8,128)S(1)} %copy-done.19, ...), custom_call_target="tpu_custom_call" | custom-call | flops 833617 | bytes 9032 | tf_op jit(solution)/shard_map/attn_back/pallas_call | solution.py:305
  174.2 6.0 %attn_weights.2 = (bf16[1,2,400,384]{3,2,1,0:T(8,128)(2,1)S(1)}, f32[8,128]{1,0:T(8,128)S(1)}) custom-call(s32[15]{0:T(128)S(1)} %concatenate.9.marks, bf16[320,768]{1,0:T(8,128)(2,1)S(1)} %get-tuple-element.347.refs_0_, bf16[320,768]{1,0:T(8,128)(2,1)S(1)} %get-tuple-element.361.refs_0_.refs_1_, bf16[320,768]{1,0:T(8,128)(2,1)S(1)} %get-tuple-element.359.refs_0_.refs_2_, ...), custom_call_target="tpu_custom_call" | custom-call | flops 614400 | bytes 400 | tf_op jit(solution)/shard_map/attn_weights/pallas_call | solution.py:476
  184.7 14.4 %attn_weights.3 = (bf16[7,2,400,384]{3,2,1,0:T(8,128)(2,1)S(1)}, f32[8,128]{1,0:T(8,128)S(1)}) custom-call(s32[15]{0:T(128)S(1)} %concatenate.9.marks, bf16[320,768]{1,0:T(8,128)(2,1)S(1)} %get-tuple-element.347.refs_0_, bf16[320,768]{1,0:T(8,128)(2,1)S(1)} %get-tuple-element.361.refs_0_.refs_1_, bf16[320,768]{1,0:T(8,128)(2,1)S(1)} %get-tuple-element.359.refs_0_.refs_2_, ...), custom_call_target="tpu_custom_call" | custom-call | flops 4300800 | bytes 2800 | tf_op jit(solution)/shard_map/attn_weights/pallas_call | solution.py:476
  201.3 5.3 %collective-permute-done.46.refs_0_ = bf16[400,384]{1,0:T(8,128)(2,1)S(1)} collective-permute-done((bf16[400,384]{1,0:T(8,128)(2,1)S(1)}, bf16[400,384]{1,0:T(8,128)(2,1)S(1)}, u32[]{:S(2)}, u32[]{:S(2)}) %collective-permute-start.46) | collective-permute-done | bytes 307232 | tf_op jit(solution)/shard_map/ppermute | solution.py:649
  212.6 5.8 %collective-permute-done.48.refs_0_ = bf16[400,384]{1,0:T(8,128)(2,1)S(1)} collective-permute-done((bf16[400,384]{1,0:T(8,128)(2,1)S(1)}, bf16[400,384]{1,0:T(8,128)(2,1)S(1)}, u32[]{:S(2)}, u32[]{:S(2)}) %collective-permute-start.48) | collective-permute-done | bytes 307232 | tf_op jit(solution)/shard_map/ppermute | solution.py:649
  222.2 11.4 %collective-permute-done.52.refs_0_ = bf16[400,384]{1,0:T(8,128)(2,1)S(1)} collective-permute-done((bf16[400,384]{1,0:T(8,128)(2,1)S(1)}, bf16[400,384]{1,0:T(8,128)(2,1)S(1)}, u32[]{:S(2)}, u32[]{:S(2)}) %collective-permute-start.52) | collective-permute-done | bytes 307232 | tf_op jit(solution)/shard_map/ppermute | solution.py:649
  239.4 14.6 %collective-permute-done.54.refs_0_ = bf16[400,384]{1,0:T(8,128)(2,1)S(1)} collective-permute-done((bf16[400,384]{1,0:T(8,128)(2,1)S(1)}, bf16[400,384]{1,0:T(8,128)(2,1)S(1)}, u32[]{:S(2)}, u32[]{:S(2)}) %collective-permute-start.54) | collective-permute-done | bytes 307232 | tf_op jit(solution)/shard_map/ppermute | solution.py:649
  259.7 14.6 %collective-permute-done.58.refs_0_ = bf16[400,384]{1,0:T(8,128)(2,1)S(1)} collective-permute-done((bf16[400,384]{1,0:T(8,128)(2,1)S(1)}, bf16[400,384]{1,0:T(8,128)(2,1)S(1)}, u32[]{:S(2)}, u32[]{:S(2)}) %collective-permute-start.58) | collective-permute-done | bytes 307232 | tf_op jit(solution)/shard_map/ppermute | solution.py:649
  281.9 10.5 %collective-permute-done.62.refs_0_ = bf16[400,384]{1,0:T(8,128)(2,1)S(1)} collective-permute-done((bf16[400,384]{1,0:T(8,128)(2,1)S(1)}, bf16[400,384]{1,0:T(8,128)(2,1)S(1)}, u32[]{:S(2)}, u32[]{:S(2)}) %collective-permute-start.62) | collective-permute-done | bytes 307232 | tf_op jit(solution)/shard_map/ppermute | solution.py:649
  302.1 10.6 %collective-permute-done.66.ahead = bf16[400,384]{1,0:T(8,128)(2,1)S(1)} collective-permute-done((bf16[400,384]{1,0:T(8,128)(2,1)S(1)}, bf16[400,384]{1,0:T(8,128)(2,1)S(1)}, u32[]{:S(2)}, u32[]{:S(2)}) %collective-permute-start.66) | collective-permute-done | bytes 307232 | tf_op jit(solution)/shard_map/ppermute | solution.py:649
  322.3 10.7 %collective-permute-done.70.ahead = bf16[400,384]{1,0:T(8,128)(2,1)S(1)} collective-permute-done((bf16[400,384]{1,0:T(8,128)(2,1)S(1)}, bf16[400,384]{1,0:T(8,128)(2,1)S(1)}, u32[]{:S(2)}, u32[]{:S(2)}) %collective-permute-start.70) | collective-permute-done | bytes 307232 | tf_op jit(solution)/shard_map/ppermute | solution.py:649
  342.5 10.8 %collective-permute-done.74.ahead = bf16[400,384]{1,0:T(8,128)(2,1)S(1)} collective-permute-done((bf16[400,384]{1,0:T(8,128)(2,1)S(1)}, bf16[400,384]{1,0:T(8,128)(2,1)S(1)}, u32[]{:S(2)}, u32[]{:S(2)}) %collective-permute-start.74) | collective-permute-done | bytes 307232 | tf_op jit(solution)/shard_map/ppermute | solution.py:649
  363.5 12.1 %collective-permute-done.78.ahead = bf16[400,384]{1,0:T(8,128)(2,1)S(1)} collective-permute-done((bf16[400,384]{1,0:T(8,128)(2,1)S(1)}, bf16[400,384]{1,0:T(8,128)(2,1)S(1)}, u32[]{:S(2)}, u32[]{:S(2)}) %collective-permute-start.78) | collective-permute-done | bytes 307232 | tf_op jit(solution)/shard_map/ppermute | solution.py:649
  387.6 6.1 %collective-permute-done.82.ahead = bf16[400,384]{1,0:T(8,128)(2,1)S(1)} collective-permute-done((bf16[400,384]{1,0:T(8,128)(2,1)S(1)}, bf16[400,384]{1,0:T(8,128)(2,1)S(1)}, u32[]{:S(2)}, u32[]{:S(2)}) %collective-permute-start.82) | collective-permute-done | bytes 307232 | tf_op jit(solution)/shard_map/ppermute | solution.py:649
  410.1 6.6 %collective-permute-done.92.ahead = bf16[768,384]{1,0:T(8,128)(2,1)S(1)} collective-permute-done((bf16[768,384]{1,0:T(8,128)(2,1)S(1)}, bf16[768,384]{1,0:T(8,128)(2,1)S(1)}, u32[]{:S(2)}, u32[]{:S(2)}) %collective-permute-start.92) | collective-permute-done | bytes 589856 | tf_op jit(solution)/shard_map/ppermute | solution.py:649
  (341 shorter events, 222.5 us)
Async XLA Ops:
  130.3 20.1 %collective-permute-start.33 = (bf16[768,384]{1,0:T(8,128)(2,1)S(1)}, bf16[768,384]{1,0:T(8,128)(2,1)S(1)}, u32[]{:S(2)}, u32[]{:S(2)}) collective-permute-start(bf16[768,384]{1,0:T(8,128)(2,1)S(1)} %get-tuple-element.639), channel_id=1, source_target_pairs={{0,4},{4,8},{8,12},{12,14},{14,10},{10,6},{6,2},{2,0},{1,5},{5,9},... | collective-permute-start | bytes 1769480 | tf_op jit(solution)/shard_map/ppermute | solution.py:649
  131.9 18.5 %collective-permute-start.34 = (bf16[768,384]{1,0:T(8,128)(2,1)S(1)}, bf16[768,384]{1,0:T(8,128)(2,1)S(1)}, u32[]{:S(2)}, u32[]{:S(2)}) collective-permute-start(bf16[768,384]{1,0:T(8,128)(2,1)S(1)} %get-tuple-element.638), channel_id=1, source_target_pairs={{4,0},{8,4},{12,8},{14,12},{10,14},{6,10},{2,6},{0,2},{5,1},{9,5},... | collective-permute-start | bytes 1769480 | tf_op jit(solution)/shard_map/ppermute | solution.py:649
  180.2 18.8 %collective-permute-start.42 = (bf16[400,384]{1,0:T(8,128)(2,1)S(1)}, bf16[400,384]{1,0:T(8,128)(2,1)S(1)}, u32[]{:S(2)}, u32[]{:S(2)}) collective-permute-start(bf16[400,384]{1,0:T(8,128)(2,1)S(1)} %get-tuple-element.641), channel_id=1, source_target_pairs={{0,4},{4,8},{8,12},{12,14},{14,10},{10,6},{6,2},{2,0},{1,5},{5,9},... | collective-permute-start | bytes 921608 | tf_op jit(solution)/shard_map/ppermute | solution.py:649
  182.6 27.7 %collective-permute-start.50 = (bf16[768,384]{1,0:T(8,128)(2,1)S(1)}, bf16[768,384]{1,0:T(8,128)(2,1)S(1)}, u32[]{:S(2)}, u32[]{:S(2)}) collective-permute-start(bf16[768,384]{1,0:T(8,128)(2,1)S(1)} %get-tuple-element.479), channel_id=1, source_target_pairs={{0,4},{4,8},{8,12},{12,14},{14,10},{10,6},{6,2},{2,0},{1,5},{5,9},... | collective-permute-start | bytes 1769480 | tf_op jit(solution)/shard_map/ppermute | solution.py:649
  184.5 25.8 %collective-permute-start.51 = (bf16[768,384]{1,0:T(8,128)(2,1)S(1)}, bf16[768,384]{1,0:T(8,128)(2,1)S(1)}, u32[]{:S(2)}, u32[]{:S(2)}) collective-permute-start(bf16[768,384]{1,0:T(8,128)(2,1)S(1)} %get-tuple-element.480), channel_id=1, source_target_pairs={{4,0},{8,4},{12,8},{14,12},{10,14},{6,10},{2,6},{0,2},{5,1},{9,5},... | collective-permute-start | bytes 1769480 | tf_op jit(solution)/shard_map/ppermute | solution.py:649
  210.6 24.4 %collective-permute-start.56 = (bf16[768,384]{1,0:T(8,128)(2,1)S(1)}, bf16[768,384]{1,0:T(8,128)(2,1)S(1)}, u32[]{:S(2)}, u32[]{:S(2)}) collective-permute-start(bf16[768,384]{1,0:T(8,128)(2,1)S(1)} %get-tuple-element.497), channel_id=1, source_target_pairs={{0,4},{4,8},{8,12},{12,14},{14,10},{10,6},{6,2},{2,0},{1,5},{5,9},... | collective-permute-start | bytes 1769480 | tf_op jit(solution)/shard_map/ppermute | solution.py:649
  212.1 22.9 %collective-permute-start.57 = (bf16[768,384]{1,0:T(8,128)(2,1)S(1)}, bf16[768,384]{1,0:T(8,128)(2,1)S(1)}, u32[]{:S(2)}, u32[]{:S(2)}) collective-permute-start(bf16[768,384]{1,0:T(8,128)(2,1)S(1)} %get-tuple-element.498), channel_id=1, source_target_pairs={{4,0},{8,4},{12,8},{14,12},{10,14},{6,10},{2,6},{0,2},{5,1},{9,5},... | collective-permute-start | bytes 1769480 | tf_op jit(solution)/shard_map/ppermute | solution.py:649
  235.3 19.9 %collective-permute-start.60 = (bf16[768,384]{1,0:T(8,128)(2,1)S(1)}, bf16[768,384]{1,0:T(8,128)(2,1)S(1)}, u32[]{:S(2)}, u32[]{:S(2)}) collective-permute-start(bf16[768,384]{1,0:T(8,128)(2,1)S(1)} %get-tuple-element.509), channel_id=1, source_target_pairs={{0,4},{4,8},{8,12},{12,14},{14,10},{10,6},{6,2},{2,0},{1,5},{5,9},... | collective-permute-start | bytes 1769480 | tf_op jit(solution)/shard_map/ppermute | solution.py:649
  236.8 18.4 %collective-permute-start.61 = (bf16[768,384]{1,0:T(8,128)(2,1)S(1)}, bf16[768,384]{1,0:T(8,128)(2,1)S(1)}, u32[]{:S(2)}, u32[]{:S(2)}) collective-permute-start(bf16[768,384]{1,0:T(8,128)(2,1)S(1)} %get-tuple-element.510), channel_id=1, source_target_pairs={{4,0},{8,4},{12,8},{14,12},{10,14},{6,10},{2,6},{0,2},{5,1},{9,5},... | collective-permute-start | bytes 1769480 | tf_op jit(solution)/shard_map/ppermute | solution.py:649
  255.6 19.9 %collective-permute-start.64 = (bf16[768,384]{1,0:T(8,128)(2,1)S(1)}, bf16[768,384]{1,0:T(8,128)(2,1)S(1)}, u32[]{:S(2)}, u32[]{:S(2)}) collective-permute-start(bf16[768,384]{1,0:T(8,128)(2,1)S(1)} %get-tuple-element.521), channel_id=1, source_target_pairs={{0,4},{4,8},{8,12},{12,14},{14,10},{10,6},{6,2},{2,0},{1,5},{5,9},... | collective-permute-start | bytes 1769480 | tf_op jit(solution)/shard_map/ppermute | solution.py:649
  257.1 18.4 %collective-permute-start.65 = (bf16[768,384]{1,0:T(8,128)(2,1)S(1)}, bf16[768,384]{1,0:T(8,128)(2,1)S(1)}, u32[]{:S(2)}, u32[]{:S(2)}) collective-permute-start(bf16[768,384]{1,0:T(8,128)(2,1)S(1)} %get-tuple-element.522), channel_id=1, source_target_pairs={{4,0},{8,4},{12,8},{14,12},{10,14},{6,10},{2,6},{0,2},{5,1},{9,5},... | collective-permute-start | bytes 1769480 | tf_op jit(solution)/shard_map/ppermute | solution.py:649
  275.8 20.2 %collective-permute-start.68 = (bf16[768,384]{1,0:T(8,128)(2,1)S(1)}, bf16[768,384]{1,0:T(8,128)(2,1)S(1)}, u32[]{:S(2)}, u32[]{:S(2)}) collective-permute-start(bf16[768,384]{1,0:T(8,128)(2,1)S(1)} %get-tuple-element.527.ahead), channel_id=1, source_target_pairs={{0,4},{4,8},{8,12},{12,14},{14,10},{10,6},{6,2},{2,0},{1,5},{5,9},... | collective-permute-start | bytes 1769480 | tf_op jit(solution)/shard_map/ppermute | solution.py:649
  277.3 18.7 %collective-permute-start.69 = (bf16[768,384]{1,0:T(8,128)(2,1)S(1)}, bf16[768,384]{1,0:T(8,128)(2,1)S(1)}, u32[]{:S(2)}, u32[]{:S(2)}) collective-permute-start(bf16[768,384]{1,0:T(8,128)(2,1)S(1)} %get-tuple-element.528.back), channel_id=1, source_target_pairs={{4,0},{8,4},{12,8},{14,12},{10,14},{6,10},{2,6},{0,2},{5,1},{9,5},... | collective-permute-start | bytes 1769480 | tf_op jit(solution)/shard_map/ppermute | solution.py:649
  296.0 20.2 %collective-permute-start.72 = (bf16[768,384]{1,0:T(8,128)(2,1)S(1)}, bf16[768,384]{1,0:T(8,128)(2,1)S(1)}, u32[]{:S(2)}, u32[]{:S(2)}) collective-permute-start(bf16[768,384]{1,0:T(8,128)(2,1)S(1)} %collective-permute-done.68.ahead), channel_id=1, source_target_pairs={{0,4},{4,8},{8,12},{12,14},{14,10},{10,6},{6,2},{2,0},{1,5},{5,9},... | collective-permute-start | bytes 1769480 | tf_op jit(solution)/shard_map/ppermute | solution.py:649
  297.4 18.7 %collective-permute-start.73 = (bf16[768,384]{1,0:T(8,128)(2,1)S(1)}, bf16[768,384]{1,0:T(8,128)(2,1)S(1)}, u32[]{:S(2)}, u32[]{:S(2)}) collective-permute-start(bf16[768,384]{1,0:T(8,128)(2,1)S(1)} %collective-permute-done.69.back), channel_id=1, source_target_pairs={{4,0},{8,4},{12,8},{14,12},{10,14},{6,10},{2,6},{0,2},{5,1},{9,5},... | collective-permute-start | bytes 1769480 | tf_op jit(solution)/shard_map/ppermute | solution.py:649
  316.1 20.2 %collective-permute-start.76 = (bf16[768,384]{1,0:T(8,128)(2,1)S(1)}, bf16[768,384]{1,0:T(8,128)(2,1)S(1)}, u32[]{:S(2)}, u32[]{:S(2)}) collective-permute-start(bf16[768,384]{1,0:T(8,128)(2,1)S(1)} %collective-permute-done.72.ahead), channel_id=1, source_target_pairs={{0,4},{4,8},{8,12},{12,14},{14,10},{10,6},{6,2},{2,0},{1,5},{5,9},... | collective-permute-start | bytes 1769480 | tf_op jit(solution)/shard_map/ppermute | solution.py:649
  317.6 18.7 %collective-permute-start.77 = (bf16[768,384]{1,0:T(8,128)(2,1)S(1)}, bf16[768,384]{1,0:T(8,128)(2,1)S(1)}, u32[]{:S(2)}, u32[]{:S(2)}) collective-permute-start(bf16[768,384]{1,0:T(8,128)(2,1)S(1)} %collective-permute-done.73.back), channel_id=1, source_target_pairs={{4,0},{8,4},{12,8},{14,12},{10,14},{6,10},{2,6},{0,2},{5,1},{9,5},... | collective-permute-start | bytes 1769480 | tf_op jit(solution)/shard_map/ppermute | solution.py:649
  336.3 20.9 %collective-permute-start.80 = (bf16[768,384]{1,0:T(8,128)(2,1)S(1)}, bf16[768,384]{1,0:T(8,128)(2,1)S(1)}, u32[]{:S(2)}, u32[]{:S(2)}) collective-permute-start(bf16[768,384]{1,0:T(8,128)(2,1)S(1)} %collective-permute-done.76.ahead), channel_id=1, source_target_pairs={{0,4},{4,8},{8,12},{12,14},{14,10},{10,6},{6,2},{2,0},{1,5},{5,9},... | collective-permute-start | bytes 1769480 | tf_op jit(solution)/shard_map/ppermute | solution.py:649
  337.8 19.5 %collective-permute-start.81 = (bf16[768,384]{1,0:T(8,128)(2,1)S(1)}, bf16[768,384]{1,0:T(8,128)(2,1)S(1)}, u32[]{:S(2)}, u32[]{:S(2)}) collective-permute-start(bf16[768,384]{1,0:T(8,128)(2,1)S(1)} %collective-permute-done.77.back), channel_id=1, source_target_pairs={{4,0},{8,4},{12,8},{14,12},{10,14},{6,10},{2,6},{0,2},{5,1},{9,5},... | collective-permute-start | bytes 1769480 | tf_op jit(solution)/shard_map/ppermute | solution.py:649
  357.3 23.1 %collective-permute-start.84 = (bf16[768,384]{1,0:T(8,128)(2,1)S(1)}, bf16[768,384]{1,0:T(8,128)(2,1)S(1)}, u32[]{:S(2)}, u32[]{:S(2)}) collective-permute-start(bf16[768,384]{1,0:T(8,128)(2,1)S(1)} %collective-permute-done.80.ahead), channel_id=1, source_target_pairs={{0,4},{4,8},{8,12},{12,14},{14,10},{10,6},{6,2},{2,0},{1,5},{5,9},... | collective-permute-start | bytes 1769480 | tf_op jit(solution)/shard_map/ppermute | solution.py:649
  359.2 21.2 %collective-permute-start.85 = (bf16[768,384]{1,0:T(8,128)(2,1)S(1)}, bf16[768,384]{1,0:T(8,128)(2,1)S(1)}, u32[]{:S(2)}, u32[]{:S(2)}) collective-permute-start(bf16[768,384]{1,0:T(8,128)(2,1)S(1)} %collective-permute-done.81.back), channel_id=1, source_target_pairs={{4,0},{8,4},{12,8},{14,12},{10,14},{6,10},{2,6},{0,2},{5,1},{9,5},... | collective-permute-start | bytes 1769480 | tf_op jit(solution)/shard_map/ppermute | solution.py:649
  398.4 18.2 %collective-permute-start.92 = (bf16[768,384]{1,0:T(8,128)(2,1)S(1)}, bf16[768,384]{1,0:T(8,128)(2,1)S(1)}, u32[]{:S(2)}, u32[]{:S(2)}) collective-permute-start(bf16[768,384]{1,0:T(8,128)(2,1)S(1)} %collective-permute-done.88.ahead), channel_id=1, source_target_pairs={{0,4},{4,8},{8,12},{12,14},{14,10},{10,6},{6,2},{2,0},{1,5},{5,9},... | collective-permute-start | bytes 1769480 | tf_op jit(solution)/shard_map/ppermute | solution.py:649
  398.9 18.2 %collective-permute-start.93 = (bf16[768,384]{1,0:T(8,128)(2,1)S(1)}, bf16[768,384]{1,0:T(8,128)(2,1)S(1)}, u32[]{:S(2)}, u32[]{:S(2)}) collective-permute-start(bf16[768,384]{1,0:T(8,128)(2,1)S(1)} %collective-permute-done.89.back), channel_id=1, source_target_pairs={{4,0},{8,4},{12,8},{14,12},{10,14},{6,10},{2,6},{0,2},{5,1},{9,5},... | collective-permute-start | bytes 1769480 | tf_op jit(solution)/shard_map/ppermute | solution.py:649
  404.4 18.1 %collective-permute-start.90 = (bf16[400,384]{1,0:T(8,128)(2,1)S(1)}, bf16[400,384]{1,0:T(8,128)(2,1)S(1)}, u32[]{:S(2)}, u32[]{:S(2)}) collective-permute-start(bf16[400,384]{1,0:T(8,128)(2,1)S(1)} %collective-permute-done.86.ahead), channel_id=1, source_target_pairs={{0,4},{4,8},{8,12},{12,14},{14,10},{10,6},{6,2},{2,0},{1,5},{5,9},... | collective-permute-start | bytes 921608 | tf_op jit(solution)/shard_map/ppermute | solution.py:649
  (114 other events, 1208.2 us)
